TPU v7x, 512 devices: a whole 4x4x16 slice. The times are simulated.
512 devices in a mesh: grp: 8 (over z_hi, y), seq: 8 (over x, core), tp: 8 (over z_lo).
Axes of the slice: x: 4, y: 4, z: 16 (z_hi: 2, z_lo: 8; z = z_hi * 8 + z_lo), core: 2. Of those that a mesh axis runs over, the one named last changes fastest.
Arguments:
- fc_big: bfloat16 [8192, 6912], P(('grp', 'seq'), 'tp'), may hold values from -6 to 6
- fc_guide: bfloat16 [8192, 4480], P(('grp', 'seq'), 'tp'), may hold values from -6 to 6
- res_big: bfloat16 [8192, 5120], P(('grp', 'tp'), 'seq'), may hold values from -6 to 6
- res_guide: bfloat16 [8192, 1536], P(('grp', 'tp'), 'seq'), may hold values from -6 to 6
- cotangent: float32 [8192, 64], P(('grp', 'tp')), may hold values from -6 to 6
- proj_big: bfloat16 [6912, 5120], P('tp', 'seq'), may hold values from -0.078125 to 0.078125
- proj_guide: bfloat16 [4480, 1536], P('tp', 'seq'), may hold values from -0.09375 to 0.09375
- head_big: bfloat16 [5120, 64], P('seq'), may hold values from -0.078125 to 0.078125
- head_guide: bfloat16 [1536, 64], P('seq'), may hold values from -0.15625 to 0.15625
- modulation_big: float32 [50, 3, 5120], P(None, None, 'seq'), may hold values from -3 to 3
- modulation_guide: float32 [50, 3, 1536], P(None, None, 'seq'), may hold values from -3 to 3
- weight_table: float32 [8], replicated, may hold values from 1.5 to 4
- time_index: int32 [8], P('grp'), may hold values from 0 to 49
- weight_index: int32 [8], P('grp'), may hold values from 0 to 7
Outputs:
- guided: float32 [8192, 64], P(('grp', 'tp'))
- grad_proj: bfloat16 [6912, 5120], P('tp', 'seq')
- grad_head: float32 [5120, 64], P('seq')
- grad_res_big: bfloat16 [8192, 5120], P(('grp', 'tp'), 'seq')
- grad_res_guide: bfloat16 [8192, 1536], P(('grp', 'tp'), 'seq')
All inputs are finite; a program needn't handle non-finite values.
Results may differ from a plain program's by a relative error of at most 0.019.
Values may be sent and summed in bfloat16 or wider, within the bound.
A program may use at most 64 MiB of HBM per device.

v0:
```python
import jax
import jax.numpy as jnp
from jax import lax
from jax.sharding import PartitionSpec as P

DB = 5120
DG = 1536
STEPS = 50
LEVELS = 8


EPSILON = 1e-06


def lookup(hot_row, table):
    flat = jnp.dot(hot_row, table.reshape(table.shape[0], -1), precision=lax.Precision.HIGHEST)
    return flat.reshape(3, -1)


def shards(
    fc_big,
    fc_guide,
    res_big,
    res_guide,
    cotangent,
    proj_big,
    proj_guide,
    head_big,
    head_guide,
    modulation_big,
    modulation_guide,
    weight_table,
    time_index,
    weight_index,
):
    width_big = res_big.shape[1]
    full_big, full_guide = (
        lax.all_gather(fc_big, "seq", axis=0, tiled=True),
        lax.all_gather(fc_guide, "seq", axis=0, tiled=True),
    )
    term_big = jnp.dot(full_big, proj_big, preferred_element_type=jnp.float32)
    term_guide = jnp.dot(full_guide, proj_guide, preferred_element_type=jnp.float32)
    summed = lax.psum_scatter(
        jnp.concatenate([term_big, term_guide], axis=1).astype(jnp.bfloat16),
        "tp",
        scatter_dimension=0,
        tiled=True,
    ).astype(jnp.float32)
    time_hot = (jnp.arange(STEPS) == time_index[0]).astype(jnp.float32)
    level_hot = (jnp.arange(LEVELS) == weight_index[0]).astype(jnp.float32)
    strength = jnp.dot(level_hot, weight_table, precision=lax.Precision.HIGHEST)
    table_big = lookup(time_hot, modulation_big)
    table_guide = lookup(time_hot, modulation_guide)
    stream_big = res_big.astype(jnp.float32) + table_big[0] * summed[:, :width_big]
    stream_guide = res_guide.astype(jnp.float32) + table_guide[0] * summed[:, width_big:]
    totals = lax.psum((jnp.sum(stream_big, axis=1), jnp.sum(stream_guide, axis=1)), "seq")
    centred_big = stream_big - (totals[0] / DB)[:, None]
    centred_guide = stream_guide - (totals[1] / DG)[:, None]
    squares = lax.psum(
        (
            jnp.sum(centred_big * centred_big, axis=1),
            jnp.sum(centred_guide * centred_guide, axis=1),
        ),
        "seq",
    )
    variance_big = squares[0] / DB
    variance_guide = squares[1] / DG
    inverse_big = lax.rsqrt(variance_big + EPSILON)[:, None]
    inverse_guide = lax.rsqrt(variance_guide + EPSILON)[:, None]
    normed_big = centred_big * inverse_big
    normed_guide = centred_guide * inverse_guide
    shaped_big = (normed_big * (1.0 + table_big[2]) + table_big[1]).astype(jnp.bfloat16)
    shaped_guide = (normed_guide * (1.0 + table_guide[2]) + table_guide[1]).astype(jnp.bfloat16)
    product_big = jnp.dot(shaped_big, head_big, preferred_element_type=jnp.float32)
    product_guide = jnp.dot(shaped_guide, head_guide, preferred_element_type=jnp.float32)
    cot_big = (strength * cotangent).astype(jnp.bfloat16)
    cot_guide = ((1.0 - strength) * cotangent).astype(jnp.bfloat16)
    scaled_big = jnp.dot(cot_big, head_big.T, preferred_element_type=jnp.float32) * (
        1.0 + table_big[2]
    )
    scaled_guide = jnp.dot(cot_guide, head_guide.T, preferred_element_type=jnp.float32) * (
        1.0 + table_guide[2]
    )
    local_sums = (
        jnp.sum(scaled_big, axis=1),
        jnp.sum(scaled_big * normed_big, axis=1),
        jnp.sum(scaled_guide, axis=1),
        jnp.sum(scaled_guide * normed_guide, axis=1),
    )
    head_sum_big, head_sum_guide, first_big, second_big, first_guide, second_guide = (
        lax.psum(product_big.astype(jnp.bfloat16), "seq").astype(jnp.float32),
        lax.psum(product_guide.astype(jnp.bfloat16), "seq").astype(jnp.float32),
        lax.psum(local_sums[0].astype(jnp.bfloat16), "seq").astype(jnp.float32),
        lax.psum(local_sums[1].astype(jnp.bfloat16), "seq").astype(jnp.float32),
        lax.psum(local_sums[2].astype(jnp.bfloat16), "seq").astype(jnp.float32),
        lax.psum(local_sums[3].astype(jnp.bfloat16), "seq").astype(jnp.float32),
    )
    guided = head_sum_guide + strength * (head_sum_big - head_sum_guide)
    grad_big = inverse_big * (
        scaled_big - (first_big / DB)[:, None] - normed_big * (second_big / DB)[:, None]
    )
    grad_guide = inverse_guide * (
        scaled_guide - (first_guide / DG)[:, None] - normed_guide * (second_guide / DG)[:, None]
    )
    signal = (grad_big * table_big[0]).astype(jnp.bfloat16)
    group_grad = lax.dot_general(
        full_big,
        lax.all_gather(signal, "tp", axis=0, tiled=True),
        (((0,), (0,)), ((), ())),
        preferred_element_type=jnp.float32,
    )
    grad_proj = lax.psum(group_grad.astype(jnp.bfloat16), "grp")
    head_local = lax.dot_general(
        shaped_big, cot_big, (((0,), (0,)), ((), ())), preferred_element_type=jnp.float32
    )
    grad_head = lax.psum(head_local, ("grp", "tp"))
    return (
        guided,
        grad_proj,
        grad_head,
        grad_big.astype(jnp.bfloat16),
        grad_guide.astype(jnp.bfloat16),
    )


def solution(mesh):
    placed = (
        P(("grp", "seq"), "tp"),
        P(("grp", "seq"), "tp"),
        P(("grp", "tp"), "seq"),
        P(("grp", "tp"), "seq"),
        P(("grp", "tp"), None),
        P("tp", "seq"),
        P("tp", "seq"),
        P("seq", None),
        P("seq", None),
        P(None, None, "seq"),
        P(None, None, "seq"),
        P(),
        P("grp"),
        P("grp"),
    )
    return jax.shard_map(
        shards,
        mesh=mesh,
        in_specs=placed,
        out_specs=(
            P(("grp", "tp"), None),
            P("tp", "seq"),
            P("seq", None),
            P(("grp", "tp"), "seq"),
            P(("grp", "tp"), "seq"),
        ),
        check_vma=False,
    )
```

profile of v0, /device:TPU:24, one launch (start us, length us, event | category | flops | bytes accessed | tf_op | source)
XLA Modules:
  0.0 721.2 jit_solution(17122736324028606671)
XLA Ops:
  7.2 0.0 copy-start
  7.2 0.0 all-gather.6.cloned.1.call-start
  7.2 0.7 all-gather.6.cloned.1.call-update
  7.9 0.0 all-gather.4.cloned.1.call-start
  8.0 0.7 all-gather.4.cloned.1.call-update
  8.7 0.0 reduce-scatter.4.cloned.1.call-start
  8.7 37.0 %all-gather.6.cloned.1.call-done = bf16[1024,560]{0,1:T(8,128)(2,1)} async-done(((bf16[128,560]{0,1:T(8,128)(2,1)}), bf16[1024,560]{0,1:T(8,128)(2,1)}) %all-gather.6.cloned.1.call-update) | async-done | bytes 1146896 | tf_op jit(solution)/shard_map/all_gather | solution.py:39
  45.7 1.9 convolution_convert_fusion.2
  47.5 34.9 %all-gather.4.cloned.1.call-done = bf16[1024,864]{0,1:T(8,128)(2,1)} async-done(((bf16[128,864]{0,1:T(8,128)(2,1)}), bf16[1024,864]{0,1:T(8,128)(2,1)}) %all-gather.4.cloned.1.call-update) | async-done | bytes 1769488 | tf_op jit(solution)/shard_map/all_gather | solution.py:38
  82.4 0.0 copy-done
  82.4 3.0 convolution_convert_fusion
  85.5 0.1 pad_maximum_fusion
  85.6 2.5 copy.36
  88.1 0.0 reduce-scatter.4.cloned.1.call-update
  88.1 0.0 all-gather.8.cloned.1.call-start
  88.2 0.8 copy-done.4
  89.0 0.1 copy.28
  89.1 0.2 reshape.44
  89.9 0.0 copy-done.7
  89.9 0.1 copy.27
  90.0 0.0 copy-done.1
  90.0 0.0 copy-start.9
  90.0 0.1 copy.30
  90.2 0.1 pad.2
  90.3 0.0 copy-start.6
  91.0 0.0 copy-done.9
  91.0 0.7 fusion.16
  92.4 0.2 convolution_reduce_fusion.1
  92.6 0.0 copy-start.2
  92.6 0.0 copy-start.3
  92.6 0.3 convolution_reduce_fusion
  92.9 0.1 slice_add_fusion.1
  93.0 68.1 %reduce-scatter.4.cloned.1.call-done = bf16[128,832]{1,0:T(8,128)(2,1)} async-done(((bf16[1024,832]{1,0:T(8,128)(2,1)}), bf16[128,832]{1,0:T(8,128)(2,1)}) %reduce-scatter.4.cloned.1.call-update) | async-done | bytes 213008 | tf_op jit(solution)/shard_map/reduce_scatter | solution.py:43
  161.1 1.0 convert_element_type.76
  162.1 0.1 fusion.24
  162.2 0.0 copy-start.8
  162.2 0.0 copy-done.6
  162.2 0.1 fusion.22
  162.4 12.4 %all-reduce.1 = (f32[128]{0:T(128)S(1)}, f32[128]{0:T(128)S(1)}) all-reduce(f32[128]{0:T(128)S(1)} %get-tuple-element.38, f32[128]{0:T(128)S(1)} %get-tuple-element.36), channel_id=1, replica_groups=mesh['grp'=8,'seq'=8,'tp'=8] {'seq'}, use_global_device_ids=true, to_apply=%region_2.0 | all-reduce | flops 256 | bytes 2048 | tf_op jit(solution)/shard_map/psum | solution.py:56
  174.8 0.2 multiply_reduce_fusion.3
  175.0 0.2 multiply_reduce_fusion.1
  175.2 12.4 %all-reduce = (f32[128]{0:T(128)S(1)}, f32[128]{0:T(128)S(1)}) all-reduce(f32[128]{0:T(128)S(1)} %multiply_reduce_fusion.3, f32[128]{0:T(128)S(1)} %multiply_reduce_fusion.1), channel_id=1, replica_groups=mesh['grp'=8,'seq'=8,'tp'=8] {'seq'}, use_global_device_ids=true, to_apply=%region_4.0 | all-reduce | flops 256 | bytes 2048 | tf_op jit(solution)/shard_map/psum | solution.py:59
  187.6 1.0 fusion.19
  188.6 0.2 convolution_convert_fusion.3
  188.8 0.2 convolution_convert_fusion.4
  189.0 0.3 fusion.20
  189.4 23.9 %all-reduce.2 = (bf16[128,64]{0,1:T(8,128)(2,1)S(1)}, bf16[128,64]{0,1:T(8,128)(2,1)S(1)}, bf16[128]{0:T(256)(128)(2,1)S(1)}, bf16[128]{0:T(256)(128)(2,1)S(1)},...) all-reduce(bf16[128,64]{0,1:T(8,128)(2,1)S(1)} %convolution_convert, ...), channel_id=1, replica_groups=mesh['grp'=8,'seq'=8,'tp'=8] {'seq'}, use_global_device_ids=true, to_apply=%region_5.0 | all-reduce | flops 16896 | bytes 67584 | tf_op jit(solution)/shard_map/psum | solution.py:92
  213.3 0.8 fusion.21
  214.1 0.7 multiply_convert_fusion
  214.8 0.0 all-gather.8.cloned.1.call-update
  214.9 0.0 all-reduce.8.cloned.1.call-start
  214.9 1.5 fusion.9
  216.4 0.0 all-reduce.8.cloned.1.call-update
  216.4 0.0 all-reduce.6.cloned.1.call-start
  216.5 59.5 %all-gather.8.cloned.1.call-done = bf16[1024,640]{1,0:T(8,128)(2,1)} async-done(((bf16[128,640]{1,0:T(8,128)(2,1)}), bf16[1024,640]{1,0:T(8,128)(2,1)}) %all-gather.8.cloned.1.call-update) | async-done | bytes 1310736 | tf_op jit(solution)/shard_map/all_gather | solution.py:108
  276.0 4.4 fusion
  280.3 0.0 all-reduce.6.cloned.1.call-update
  280.4 0.1 multiply_convert_fusion.1
  280.5 0.7 copy.32
  281.3 1.3 convert_add_fusion
  282.6 249.7 %all-reduce.8.cloned.1.call-done = f32[640,64]{0,1:T(8,128)} async-done(((f32[640,64]{0,1:T(8,128)}), f32[640,64]{0,1:T(8,128)}) %all-reduce.8.cloned.1.call-update) | async-done | bytes 163856 | tf_op jit(solution)/shard_map/psum | solution.py:116
  532.3 179.1 %all-reduce.6.cloned.1.call-done = bf16[864,640]{1,0:T(8,128)(2,1)} async-done(((bf16[864,640]{1,0:T(8,128)(2,1)}), bf16[864,640]{1,0:T(8,128)(2,1)}) %all-reduce.6.cloned.1.call-update) | async-done | bytes 1105936 | tf_op jit(solution)/shard_map/psum | solution.py:112
  711.3 2.3 copy.43
  713.7 0.7 copy.44
  (17 shorter events, 0.1 us)
Async XLA Ops:
  7.2 75.2 %copy-start = (bf16[864,640]{1,0:T(8,128)(2,1)S(1)}, bf16[864,640]{1,0:T(8,128)(2,1)}, u32[]{:S(2)}) copy-start(bf16[864,640]{1,0:T(8,128)(2,1)} %param.19) | copy-start | bytes 3317764
  7.2 38.5 %all-gather.6.cloned.1.call-start = ((), (), s32[]{:S(2)}) async-start(), calls=%async_computation.2 | async-start | bytes 1290240 | tf_op jit(solution)/shard_map/all_gather | solution.py:39
  7.9 74.5 %all-gather.4.cloned.1.call-start = ((), (), s32[]{:S(2)}) async-start(), calls=%async_computation.1 | async-start | bytes 1990656 | tf_op jit(solution)/shard_map/all_gather | solution.py:38
  8.7 152.5 %reduce-scatter.4.cloned.1.call-start = ((), (), s32[]{:S(2)}) async-start(), calls=%async_computation.6 | async-start | bytes 2064384 | tf_op jit(solution)/shard_map/reduce_scatter | solution.py:43
  88.1 0.9 copy-start.4
  88.1 1.8 copy-start.7
  88.1 1.9 copy-start.1
  88.1 187.9 %all-gather.8.cloned.1.call-start = ((), (), s32[]{:S(2)}) async-start(), calls=%async_computation.3 | async-start | bytes 1474560 | tf_op jit(solution)/shard_map/all_gather | solution.py:108
  90.0 1.0 copy-start.9
  90.3 71.9 %copy-start.6 = (bf16[128,640]{1,0:T(8,128)(2,1)S(1)}, bf16[128,640]{1,0:T(8,128)(2,1)}, u32[]{:S(2)}) copy-start(bf16[128,640]{1,0:T(8,128)(2,1)} %param.16) | copy-start | bytes 491524
  92.6 95.0 %copy-start.2 = (bf16[640,64]{0,1:T(8,128)(2,1)S(1)}, bf16[640,64]{0,1:T(8,128)(2,1)}, u32[]{:S(2)}) copy-start(bf16[640,64]{0,1:T(8,128)(2,1)} %param.21) | copy-start | bytes 245764
  92.6 95.0 %copy-start.3 = (f32[128,64]{0,1:T(8,128)S(1)}, f32[128,64]{0,1:T(8,128)}, u32[]{:S(2)}) copy-start(f32[128,64]{0,1:T(8,128)} %param.18) | copy-start | bytes 98308
  162.2 26.6 %copy-start.8 = (bf16[192,64]{0,1:T(8,128)(2,1)S(1)}, bf16[192,64]{0,1:T(8,128)(2,1)}, u32[]{:S(2)}) copy-start(bf16[192,64]{0,1:T(8,128)(2,1)} %param.22) | copy-start | bytes 73732
  214.9 317.4 %all-reduce.8.cloned.1.call-start = ((), (), s32[]{:S(2)}) async-start(), calls=%async_computation.5 | async-start | bytes 327680 | tf_op jit(solution)/shard_map/psum | solution.py:116
  216.4 494.9 %all-reduce.6.cloned.1.call-start = ((), (), s32[]{:S(2)}) async-start(), calls=%async_computation.4 | async-start | bytes 2211840 | tf_op jit(solution)/shard_map/psum | solution.py:112
  532.3 181.4 %copy-start.5 = (f32[640,64]{0,1:T(8,128)S(1)}, f32[640,64]{0,1:T(8,128)}, u32[]{:S(2)}) copy-start(f32[640,64]{0,1:T(8,128)} %all-reduce.8.cloned.1.call-done) | copy-start | bytes 491524
Sparse Core Ops, SparseCore 0:
  10.1 35.4 all-gather.5
  47.8 34.5 all-gather.3
  88.2 72.8 reduce-scatter.3
  215.0 60.9 all-gather.7
  279.2 253.0 all-reduce.7
  535.7 175.6 all-reduce.5
where the time goes:
time: 722 us; the launch traced here: 721 us
  waiting for transfers between devices  630 us (87%)
  blocking collectives  48.8 us (7%)
  between operations  16.4 us (2%)
  matrix products  13 us (2%)
  local copies, waits for them, and re-layouts  7.7 us (1%)
    psum x1, waiting for transfers between devices, shards(): grad_head = lax.psum(head_local, ('grp', 'tp'))  250 us
    psum x1, waiting for transfers between devices, shards(): grad_proj = lax.psum(group_grad.astype(jnp.bfloat16), 'grp')  179 us
    reduce_scatter x1, waiting for transfers between devices, shards(): lax.psum_scatter(jnp.concatenate([term_big, term_guide], axis=1).astype(j...  68.1 us
    all_gather x1, waiting for transfers between devices, shards(): lax.all_gather(signal, 'tp', axis=0, tiled=True)  59.5 us
    all_gather x1, waiting for transfers between devices, shards(): lax.all_gather(fc_guide, 'seq', axis=0, tiled=True)  37 us
    all_gather x1, waiting for transfers between devices, shards(): lax.all_gather(fc_big, 'seq', axis=0, tiled=True)  34.9 us
    psum x1, blocking collectives, shards(): lax.psum(product_guide.astype(jnp.bfloat16), 'seq').astype(jnp.float32)  23.9 us
  transfers between devices with their start and end apart: 6, of which 6 were waited for; matrix products, arithmetic and copies ran while one was open for 2% of the time, Pallas kernels for 0%

commit v1 on v0

v1 whole, which is shorter than its diff:
```python
import jax
import jax.numpy as jnp
from jax import lax
from jax.experimental import pallas as pl
from jax.experimental.pallas import tpu as pltpu
from jax.sharding import PartitionSpec as P

MESH = pl.DeviceIdType.MESH
F32 = jnp.float32
BF16 = jnp.bfloat16

DB = 5120
DG = 1536
EPSILON = 1e-06

TOK = 128
WB = 640
WG = 192
HB = 864
HBP = 896
HG = 560
HGP = 640
FLAT = 832
NQ = 4
SUB = FLAT // NQ
SKEW = 3
NA = 4
ASUB = WB // NA
NC = 5
SHARD = 224
HALF = 112


def remote(src, dst, send, recv, device):
    return pltpu.make_async_remote_copy(
        src_ref=src, dst_ref=dst, send_sem=send, recv_sem=recv, device_id=device, device_id_type=MESH
    )


def kernel(
    time_ref,
    level_ref,
    table_ref,
    fc_b,
    fc_g,
    res_b,
    res_g,
    cot_ref,
    proj_b_hbm,
    proj_g_hbm,
    head_b,
    head_g,
    mod_b,
    mod_g,
    guided_ref,
    grad_proj_hbm,
    grad_head_ref,
    grad_res_b,
    grad_res_g,
    proj_b,
    proj_g,
    fc_all,
    fc_t,
    term,
    got_r,
    got_l,
    put_r,
    put_l,
    total,
    dev_b,
    dev_g,
    scaled_b,
    scaled_g,
    spread,
    cots,
    cot_t,
    stats,
    facts,
    signal,
    shaped,
    head_sum,
    parts,
    grad,
    one_a,
    one_b,
    two_a,
    two_b,
    mid_a,
    mid_b,
    zed,
    zed_in,
    final,
    heads,
    head_full,
    local_sem,
    fc_send,
    fc_recv,
    cot_send,
    cot_recv,
    r_send,
    r_recv,
    l_send,
    l_recv,
    ar_send,
    al_send,
    a_recv,
    st_send,
    st_recv,
    fa_send,
    fa_recv,
    pt_send,
    pt_recv,
    one_send,
    one_recv,
    two_send,
    two_recv,
    z_send,
    z_recv,
    g1_send,
    g1_recv,
    g2_send,
    g2_recv,
    hd_send,
    hd_recv,
    out_sem,
):
    grp = lax.axis_index("grp")
    me = lax.axis_index("seq")
    j = lax.axis_index("tp")
    y = lax.rem(grp, 4)
    zh4 = grp - y
    x = lax.div(me, 2)
    core = lax.rem(me, 2)
    y_flip = y + 1 - 2 * lax.rem(y, 2)
    y_back = 3 - y
    sib = me + 1 - 2 * core
    xr = lax.rem(x + 1, 4)
    xl = lax.rem(x + 3, 4)
    xf = lax.rem(x + 2, 4)
    dev_flip = {"grp": zh4 + y_flip}
    dev_back = {"grp": zh4 + y_back}
    dev_z = {"grp": lax.rem(grp + 4, 8)}

    def seq_peer(n):
        return lax.rem(me + n, 8)

    def tp_peer(n):
        return lax.rem(j + n, 8)

    barrier = pltpu.get_barrier_semaphore()
    for n in range(1, 8):
        pl.semaphore_signal(barrier, inc=1, device_id={"seq": seq_peer(n)}, device_id_type=MESH)
        pl.semaphore_signal(barrier, inc=1, device_id={"tp": tp_peer(n)}, device_id_type=MESH)
    for device in (dev_flip, dev_back, dev_z):
        pl.semaphore_signal(barrier, inc=1, device_id=device, device_id_type=MESH)

    load_b = pltpu.make_async_copy(proj_b_hbm, proj_b.at[pl.ds(0, HB)], local_sem.at[0])
    load_g = pltpu.make_async_copy(proj_g_hbm, proj_g.at[pl.ds(0, HG)], local_sem.at[1])
    load_b.start()
    load_g.start()
    proj_b[HB:HBP, :] = jnp.zeros((HBP - HB, WB), BF16)
    proj_g[HG:HGP, :] = jnp.zeros((HGP - HG, WG), BF16)
    fc_all[me, :, 0:HBP] = jnp.concatenate([fc_b[...], jnp.zeros((TOK, HBP - HB), BF16)], axis=1)
    fc_all[me, :, HBP : HBP + HGP] = jnp.concatenate(
        [fc_g[...], jnp.zeros((TOK, HGP - HG), BF16)], axis=1
    )
    strength = table_ref[level_ref[0]]
    when = time_ref[0]
    rows_b = mod_b[when]
    rows_g = mod_g[when]
    gate_b, shift_b, scale_b = rows_b[0:1], rows_b[1:2], 1.0 + rows_b[2:3]
    gate_g, shift_g, scale_g = rows_g[0:1], rows_g[1:2], 1.0 + rows_g[2:3]
    cot = cot_ref[...]
    cot_b = (strength * cot).astype(BF16)
    cot_g = ((1.0 - strength) * cot).astype(BF16)
    cots[j] = jnp.concatenate([cot_b[0:64], cot_b[64:128]], axis=1)
    pl.semaphore_wait(barrier, 17)

    def hidden(s, h):
        return fc_all.at[s, pl.ds(64 * h, 64)]

    def hidden_copy(s, h, k, target):
        return remote(hidden(s, h), hidden(s, h), fc_send.at[k], fc_recv.at[s, h], {"seq": target})

    to_r, to_l = 2 * xr + core, 2 * xl + core
    sent = []

    def send_hidden(s, h, k, target):
        copy = hidden_copy(s, h, k, target)
        copy.start()
        sent.append(copy)

    def wait_hidden(s, h):
        hidden_copy(s, h, 0, sib).wait_recv()

    send_hidden(me, 0, 0, to_r)
    send_hidden(me, 1, 1, to_l)
    send_hidden(me, 0, 2, sib)
    send_hidden(me, 1, 3, sib)
    send_hidden(me, 1, 4, to_r)
    send_hidden(me, 0, 5, to_l)

    for n in range(1, 8):
        p = tp_peer(n)
        copy = remote(cots.at[j], cots.at[j], cot_send.at[n], cot_recv.at[j], {"tp": p})
        copy.start()
        sent.append(copy)

    scaled_b[...] = (
        lax.dot_general(cot_b, head_b[...], (((1,), (1,)), ((), ())), preferred_element_type=F32)
        * scale_b
    )
    scaled_g[...] = (
        lax.dot_general(cot_g, head_g[...], (((1,), (1,)), ((), ())), preferred_element_type=F32)
        * scale_g
    )
    load_b.wait()
    load_g.wait()

    def terms(first, second):
        def one(i, carry):
            s = jnp.where(i == 0, first, second)
            block = fc_all[s, :, 0:HBP]
            product = jnp.dot(block, proj_b[...], preferred_element_type=F32)
            for q in range(NC):
                term[s, pl.ds(128 * q, 128), :] = product[:, 128 * q : 128 * q + 128]
            product = jnp.dot(
                fc_all[s, :, HBP : HBP + HGP], proj_g[...], preferred_element_type=F32
            )
            term[s, 640:768, :] = product[:, 0:128]
            term[s, 768:832, :] = jnp.concatenate(
                [product[0:64, 128:192], product[64:128, 128:192]], axis=1
            )
            fc_t[:, pl.ds(pl.multiple_of(s * 128, 128), 128)] = block.T
            return carry

        lax.fori_loop(0, 2, one, 0)

    left, right, far = to_l, to_r, 2 * xf + core
    left_s, right_s, far_s = 2 * xl + 1 - core, 2 * xr + 1 - core, 2 * xf + 1 - core
    wait_hidden(sib, 0)
    wait_hidden(sib, 1)
    terms(me, sib)
    wait_hidden(left, 0)
    send_hidden(left, 0, 6, to_r)
    send_hidden(left, 0, 7, sib)
    wait_hidden(right, 1)
    send_hidden(right, 1, 8, to_l)
    send_hidden(right, 1, 9, sib)
    wait_hidden(left, 1)
    send_hidden(left, 1, 10, sib)
    wait_hidden(right, 0)
    send_hidden(right, 0, 11, sib)
    terms(left, right)
    for h in range(2):
        wait_hidden(left_s, h)
        wait_hidden(right_s, h)
    terms(left_s, right_s)
    wait_hidden(far, 0)
    send_hidden(far, 0, 12, sib)
    wait_hidden(far, 1)
    send_hidden(far, 1, 13, sib)
    wait_hidden(far_s, 0)
    wait_hidden(far_s, 1)
    terms(far, far_s)

    def piece(q):
        return pl.ds(pl.multiple_of(q * SUB, 16), SUB)

    def sum_copy(right_way, i, q):
        if right_way:
            return remote(
                put_r.at[i, piece(q)], got_r.at[i, piece(q)], r_send.at[i, q], r_recv.at[i, q], {"tp": j + 1}
            )
        return remote(
            put_l.at[i, piece(q)], got_l.at[i, piece(q)], l_send.at[i, q], l_recv.at[i, q], {"tp": j - 1}
        )

    def tick(t, carry):
        for right_way in (True, False):
            place = j if right_way else 7 - j
            u = t - SKEW * place
            put, got = (put_r, got_r) if right_way else (put_l, got_l)

            @pl.when((u >= 0) & (u < (7 - place) * NQ))
            def _():
                i = lax.div(u, NQ)
                q = lax.rem(u, NQ)
                d = 7 - i if right_way else i
                own = term[d, piece(q), :]

                @pl.when(place > 0)
                def _():
                    sum_copy(right_way, i, q).wait_recv()
                    put[i, piece(q), :] = (got[i, piece(q), :].astype(F32) + own).astype(BF16)

                @pl.when(place == 0)
                def _():
                    put[i, piece(q), :] = own.astype(BF16)

                sum_copy(right_way, i, q).start()

        return carry

    lax.fori_loop(0, 7 * NQ + 7 * SKEW, tick, 0)

    total[...] = term[j]
    for right_way in (True, False):
        place = j if right_way else 7 - j
        got = got_r if right_way else got_l

        @pl.when(place > 0)
        def _():
            for q in range(NQ):
                sum_copy(right_way, 7 - place, q).wait_recv()
            total[...] += got[7 - place].astype(F32)

    summed_b = jnp.concatenate([total[128 * q : 128 * q + 128, :] for q in range(NC)], axis=1)
    stream_b = res_b[...].astype(F32) + gate_b * summed_b
    mean_b = jnp.sum(stream_b, axis=1, keepdims=True) * (1.0 / WB)
    away_b = stream_b - mean_b
    for q in range(NC):
        spread[j, 128 * q : 128 * q + 128, :] = away_b[:, 128 * q : 128 * q + 128].astype(BF16)
    dev_b[...] = away_b

    def a_piece(q):
        return pl.ds(q * ASUB, ASUB)

    def a_copy(right_way, k, q):
        if right_way:
            return remote(
                spread.at[k, a_piece(q)], spread.at[k, a_piece(q)], ar_send.at[k, q], a_recv.at[k, q], {"tp": j + 1}
            )
        return remote(
            spread.at[k, a_piece(q)], spread.at[k, a_piece(q)], al_send.at[k, q], a_recv.at[k, q], {"tp": j - 1}
        )

    def forward(i):
        for q in range(NA):
            for right_way in (True, False):
                place = j if right_way else 7 - j
                k = j - i if right_way else j + i

                @pl.when(place >= i)
                def _():
                    @pl.when(i > 0)
                    def _():
                        a_copy(right_way, k, q).wait_recv()

                    @pl.when(place < 7)
                    def _():
                        a_copy(right_way, k, q).start()

    forward(jnp.int32(0))

    tail_g = total[768:832, :]
    summed_g = jnp.concatenate(
        [total[640:768, :], jnp.concatenate([tail_g[:, 0:64], tail_g[:, 64:128]], axis=0)], axis=1
    )
    stream_g = res_g[...].astype(F32) + gate_g * summed_g
    mean_g = jnp.sum(stream_g, axis=1, keepdims=True) * (1.0 / WG)
    away_g = stream_g - mean_g
    dev_g[...] = away_g
    up_b, up_g = scaled_b[...], scaled_g[...]
    columns = (
        mean_b,
        jnp.sum(away_b * away_b, axis=1, keepdims=True),
        jnp.sum(up_b, axis=1, keepdims=True),
        jnp.sum(up_b * away_b, axis=1, keepdims=True),
        mean_g,
        jnp.sum(away_g * away_g, axis=1, keepdims=True),
        jnp.sum(up_g, axis=1, keepdims=True),
        jnp.sum(up_g * away_g, axis=1, keepdims=True),
    )
    lane = lax.broadcasted_iota(jnp.int32, (TOK, 128), 1)
    square = jnp.zeros((TOK, 128), F32)
    for n, column in enumerate(columns):
        square = jnp.where(lane == n, column, square)
    stats[me] = square.T[0:8]
    for n in range(1, 8):
        copy = remote(stats.at[me], stats.at[me], st_send.at[n], st_recv.at[me], {"seq": seq_peer(n)})
        copy.start()
        sent.append(copy)

    forward(jnp.int32(1))

    for n in range(1, 8):
        p = tp_peer(n)
        remote(cots.at[p], cots.at[p], cot_send.at[0], cot_recv.at[p], {"tp": p}).wait_recv()
    for n in range(1, 8):
        p = seq_peer(n)
        remote(stats.at[p], stats.at[p], st_send.at[0], st_recv.at[p], {"seq": p}).wait_recv()

    mine = stats[me]

    def norm(base, width, whole):
        every = [stats[s] for s in range(8)]
        centre = sum(r[base : base + 1] for r in every) * (1.0 / 8)
        gaps = [r[base : base + 1] - centre for r in every]
        square_sum = sum(r[base + 1 : base + 2] + width * (g * g) for r, g in zip(every, gaps))
        inverse = lax.rsqrt(square_sum * (1.0 / whole) + EPSILON)
        first = sum(r[base + 2 : base + 3] for r in every) * (1.0 / whole)
        cross = sum(r[base + 3 : base + 4] + r[base + 2 : base + 3] * g for r, g in zip(every, gaps))
        second = inverse * cross * (1.0 / whole)
        offset = inverse * (mine[base : base + 1] - centre)
        return inverse, offset, inverse * inverse * second, inverse * (first + offset * second)

    norm_b = norm(0, float(WB), float(DB))
    norm_g = norm(4, float(WG), float(DG))
    facts[j] = jnp.concatenate(norm_b + norm_g, axis=0)
    for n in range(1, 8):
        copy = remote(facts.at[j], facts.at[j], fa_send.at[n], fa_recv.at[j], {"tp": tp_peer(n)})
        copy.start()
        sent.append(copy)

    def as_columns(rows):
        return jnp.concatenate([rows, jnp.zeros((120, 128), F32)], axis=0).T

    head_sum[...] = jnp.zeros_like(head_sum)

    def consume(k):
        @pl.when(k != j)
        def _():
            remote(facts.at[k], facts.at[k], fa_send.at[0], fa_recv.at[k], {"tp": k}).wait_recv()

        turned = as_columns(facts[k])
        inverse, offset, slope, base = (turned[:, n : n + 1] for n in range(4))
        packed = cots[k].astype(F32)
        cot_k = jnp.concatenate([packed[:, 0:64], packed[:, 64:128]], axis=0)
        up = lax.dot_general(
            cot_k.astype(BF16), head_b[...], (((1,), (1,)), ((), ())), preferred_element_type=F32
        )
        away = jnp.concatenate(
            [spread[k, 128 * q : 128 * q + 128, :] for q in range(NC)], axis=1
        ).astype(F32)
        signal[pl.ds(pl.multiple_of(k * 128, 128), 128), :] = (
            gate_b * (inverse * (up * scale_b) - slope * away - base)
        ).astype(BF16)
        shaped_k = ((inverse * away + offset) * scale_b + shift_b).astype(BF16)
        shaped[...] = shaped_k
        head_sum[...] += jnp.dot(
            cot_k.T.astype(BF16), shaped_k, preferred_element_type=F32
        )

    def consume_both(i):
        @pl.when(j >= i)
        def _():
            consume(j - i)

        @pl.when((j + i <= 7) & (i > 0))
        def _():
            consume(j + i)

    def step(i, carry):
        @pl.when(i < 8)
        def _():
            forward(i)

        consume_both(i - 2)
        return carry

    lax.fori_loop(2, 10, step, 0)

    def rows(shard, half):
        return pl.ds(pl.multiple_of(shard * SHARD + half * HALF, 16), HALF)

    def one_copies(c):
        return [
            remote(grad.at[c, rows(y_flip, 0)], one_a.at[c, 0], one_send.at[c, 0], one_recv.at[c, 0], dev_flip),
            remote(grad.at[c, rows(3 - y_flip, 0)], one_a.at[c, 1], one_send.at[c, 1], one_recv.at[c, 1], dev_flip),
            remote(grad.at[c, rows(y_back, 1)], one_b.at[c, 0], one_send.at[c, 2], one_recv.at[c, 2], dev_back),
            remote(grad.at[c, rows(3 - y_flip, 1)], one_b.at[c, 1], one_send.at[c, 3], one_recv.at[c, 3], dev_back),
        ]

    def two_copies(c):
        return [
            remote(mid_a.at[c, 1], two_a.at[c], two_send.at[c, 0], two_recv.at[c, 0], dev_back),
            remote(mid_b.at[c, 1], two_b.at[c], two_send.at[c, 1], two_recv.at[c, 1], dev_flip),
        ]

    def z_copy(c):
        return remote(zed.at[c], zed_in.at[c], z_send.at[c], z_recv.at[c], dev_z)

    def back_one(c):
        a, b = final.at[c, rows(y, 0)], final.at[c, rows(y, 1)]
        return [
            remote(a, a, g1_send.at[c, 0], g1_recv.at[c, 0], dev_back),
            remote(b, b, g1_send.at[c, 1], g1_recv.at[c, 1], dev_flip),
        ]

    def back_two(c):
        shards = [(y, 0, dev_flip), (y_back, 0, dev_flip), (y, 1, dev_back), (y_flip, 1, dev_back)]
        out = []
        for n, (shard, half, device) in enumerate(shards):
            ref = final.at[c, rows(shard, half)]
            out.append(remote(ref, ref, g2_send.at[c, n], g2_recv.at[c, n], device))
        return out

    def add(a, b):
        return (a.astype(F32) + b.astype(F32)).astype(BF16)

    patch_rows = head_sum[pl.ds(pl.multiple_of(j * 8, 8), 8), :]
    spare = [patch_rows[:, 128 * q : 128 * q + 128] for q in range(NC)]
    spare = [
        jnp.concatenate(spare[0:4], axis=0),
        jnp.concatenate([spare[4], jnp.zeros((24, 128), F32)], axis=0),
    ]
    for t in range(NC + 2):
        if t < NC:
            c = t
            grad[c] = jnp.dot(
                fc_t[...], signal[:, 128 * c : 128 * c + 128], preferred_element_type=F32
            ).astype(BF16)
            if c < 2:
                grad[c, HB:HBP, :] = spare[c].astype(BF16)
            for copy in one_copies(c):
                copy.start()
                sent.append(copy)
        if 0 <= t - 1 < NC:
            c = t - 1
            for copy in one_copies(c):
                copy.wait_recv()
            mid_a[c, 0] = add(grad[c, rows(y, 0), :], one_a[c, 0])
            mid_a[c, 1] = add(grad[c, rows(y_back, 0), :], one_a[c, 1])
            mid_b[c, 0] = add(grad[c, rows(y, 1), :], one_b[c, 0])
            mid_b[c, 1] = add(grad[c, rows(y_flip, 1), :], one_b[c, 1])
            for copy in two_copies(c):
                copy.start()
                sent.append(copy)
        if 0 <= t - 2 < NC:
            c = t - 2
            for copy in two_copies(c):
                copy.wait_recv()
            zed[c, 0:HALF, :] = add(mid_a[c, 0], two_a[c])
            zed[c, HALF:SHARD, :] = add(mid_b[c, 0], two_b[c])
            copy = z_copy(c)
            copy.start()
            sent.append(copy)

    turned = as_columns(facts[j])
    inv_b, off_b, slope_b, base_b, inv_g, off_g, slope_g, base_g = (turned[:, n : n + 1] for n in range(8))
    grad_res_b[...] = (inv_b * scaled_b[...] - slope_b * dev_b[...] - base_b).astype(BF16)
    grad_res_g[...] = (inv_g * scaled_g[...] - slope_g * dev_g[...] - base_g).astype(BF16)
    shaped_b = ((inv_b * dev_b[...] + off_b) * scale_b + shift_b).astype(BF16)
    shaped_g = ((inv_g * dev_g[...] + off_g) * scale_g + shift_g).astype(BF16)
    part = strength * jnp.dot(shaped_b, head_b[...], preferred_element_type=F32) + (
        1.0 - strength
    ) * jnp.dot(shaped_g, head_g[...], preferred_element_type=F32)
    parts[me] = jnp.concatenate([part[0:64], part[64:128]], axis=1).astype(BF16)
    for n in range(1, 8):
        copy = remote(parts.at[me], parts.at[me], pt_send.at[n], pt_recv.at[me], {"seq": seq_peer(n)})
        copy.start()
        sent.append(copy)

    outs = []
    for t in range(NC + 2):
        if t < NC:
            c = t
            z_copy(c).wait_recv()
            final[c, pl.ds(pl.multiple_of(y * SHARD, 16), SHARD), :] = add(zed[c], zed_in[c])
            for copy in back_one(c):
                copy.start()
                sent.append(copy)
        if 0 <= t - 1 < NC:
            c = t - 1
            for copy in back_one(c):
                copy.wait_recv()
            for copy in back_two(c):
                copy.start()
                sent.append(copy)
        if 0 <= t - 2 < NC:
            c = t - 2
            for copy in back_two(c):
                copy.wait_recv()
            copy = pltpu.make_async_copy(
                final.at[c, pl.ds(0, HB)], grad_proj_hbm.at[:, pl.ds(128 * c, 128)], out_sem.at[c]
            )
            copy.start()
            outs.append(copy)
            if c == 1:
                heads[j, 0:32, :] = final[0, HB:HBP, :]
                heads[j, 32:64, :] = final[1, HB:HBP, :]
                for n in range(1, 8):
                    copy = remote(
                        heads.at[j], heads.at[j], hd_send.at[n], hd_recv.at[j], {"tp": tp_peer(n)}
                    )
                    copy.start()
                    sent.append(copy)
        if t == NC - 1:
            for n in range(1, 8):
                p = seq_peer(n)
                remote(parts.at[p], parts.at[p], pt_send.at[0], pt_recv.at[p], {"seq": p}).wait_recv()
            whole = sum(parts[s].astype(F32) for s in range(8))
            guided_ref[...] = jnp.concatenate([whole[:, 0:64], whole[:, 64:128]], axis=0)

    for n in range(1, 8):
        p = tp_peer(n)
        remote(heads.at[p], heads.at[p], hd_send.at[0], hd_recv.at[p], {"tp": p}).wait_recv()
    for p in range(8):
        block = heads[p].astype(F32)
        for q in range(NC):
            head_full[8 * p : 8 * p + 8, 128 * q : 128 * q + 128] = block[8 * q : 8 * q + 8]
    for q in range(NC):
        grad_head_ref[128 * q : 128 * q + 128, :] = head_full[:, 128 * q : 128 * q + 128].T

    for copy in outs:
        copy.wait()
    for copy in sent:
        copy.wait_send()

    def drain(t, carry):
        i = lax.div(t, NQ)
        q = lax.rem(t, NQ)
        for right_way in (True, False):
            place = j if right_way else 7 - j

            @pl.when(i < 7 - place)
            def _():
                sum_copy(right_way, i, q).wait_send()

        return carry

    lax.fori_loop(0, 7 * NQ, drain, 0)

    def drain_all(i, carry):
        for right_way in (True, False):
            place = j if right_way else 7 - j
            k = j - i if right_way else j + i

            @pl.when((place >= i) & (place < 7))
            def _():
                for q in range(NA):
                    a_copy(right_way, k, q).wait_send()

        return carry

    lax.fori_loop(0, 8, drain_all, 0)


def shards(
    fc_big,
    fc_guide,
    res_big,
    res_guide,
    cotangent,
    proj_big,
    proj_guide,
    head_big,
    head_guide,
    modulation_big,
    modulation_guide,
    weight_table,
    time_index,
    weight_index,
):
    smem = pl.BlockSpec(memory_space=pltpu.SMEM)
    vmem = pl.BlockSpec(memory_space=pltpu.VMEM)
    hbm = pl.BlockSpec(memory_space=pl.ANY)
    dma = pltpu.SemaphoreType.DMA
    V = pltpu.VMEM
    return pl.pallas_call(
        kernel,
        out_shape=(
            jax.ShapeDtypeStruct((TOK, 64), F32),
            jax.ShapeDtypeStruct((HB, WB), BF16),
            jax.ShapeDtypeStruct((WB, 64), F32),
            jax.ShapeDtypeStruct((TOK, WB), BF16),
            jax.ShapeDtypeStruct((TOK, WG), BF16),
        ),
        in_specs=[smem, smem, smem, vmem, vmem, vmem, vmem, vmem, hbm, hbm, vmem, vmem, vmem, vmem],
        out_specs=(vmem, hbm, vmem, vmem, vmem),
        scratch_shapes=[
            V((HBP, WB), BF16),
            V((HGP, WG), BF16),
            V((8, TOK, HBP + HGP), BF16),
            V((HBP, 1024), BF16),
            V((8, FLAT, 128), F32),
            V((7, FLAT, 128), BF16),
            V((7, FLAT, 128), BF16),
            V((7, FLAT, 128), BF16),
            V((7, FLAT, 128), BF16),
            V((FLAT, 128), F32),
            V((TOK, WB), F32),
            V((TOK, WG), F32),
            V((TOK, WB), F32),
            V((TOK, WG), F32),
            V((8, WB, 128), BF16),
            V((8, 64, 128), BF16),
            V((64, 128), BF16),
            V((8, 8, 128), F32),
            V((8, 8, 128), F32),
            V((1024, WB), BF16),
            V((TOK, WB), BF16),
            V((64, WB), F32),
            V((8, 64, 128), BF16),
            V((NC, HBP, 128), BF16),
            V((NC, 2, HALF, 128), BF16),
            V((NC, 2, HALF, 128), BF16),
            V((NC, HALF, 128), BF16),
            V((NC, HALF, 128), BF16),
            V((NC, 2, HALF, 128), BF16),
            V((NC, 2, HALF, 128), BF16),
            V((NC, SHARD, 128), BF16),
            V((NC, SHARD, 128), BF16),
            V((NC, HBP, 128), BF16),
            V((8, 64, 128), BF16),
            V((64, WB), F32),
            dma((2,)),
            dma((14,)),
            dma((8, 2)),
            dma((8,)),
            dma((8,)),
            dma((7, NQ)),
            dma((7, NQ)),
            dma((7, NQ)),
            dma((7, NQ)),
            dma((8, NA)),
            dma((8, NA)),
            dma((8, NA)),
            dma((8,)),
            dma((8,)),
            dma((8,)),
            dma((8,)),
            dma((8,)),
            dma((8,)),
            dma((NC, 4)),
            dma((NC, 4)),
            dma((NC, 2)),
            dma((NC, 2)),
            dma((NC,)),
            dma((NC,)),
            dma((NC, 2)),
            dma((NC, 2)),
            dma((NC, 4)),
            dma((NC, 4)),
            dma((8,)),
            dma((8,)),
            dma((NC,)),
        ],
        compiler_params=pltpu.CompilerParams(
            collective_id=0, has_side_effects=True, vmem_limit_bytes=56 * 2**20
        ),
    )(
        time_index,
        weight_index,
        weight_table,
        fc_big,
        fc_guide,
        res_big,
        res_guide,
        cotangent,
        proj_big,
        proj_guide,
        head_big,
        head_guide,
        modulation_big,
        modulation_guide,
    )


def solution(mesh):
    placed = (
        P(("grp", "seq"), "tp"),
        P(("grp", "seq"), "tp"),
        P(("grp", "tp"), "seq"),
        P(("grp", "tp"), "seq"),
        P(("grp", "tp"), None),
        P("tp", "seq"),
        P("tp", "seq"),
        P("seq", None),
        P("seq", None),
        P(None, None, "seq"),
        P(None, None, "seq"),
        P(),
        P("grp"),
        P("grp"),
    )
    return jax.shard_map(
        shards,
        mesh=mesh,
        in_specs=placed,
        out_specs=(
            P(("grp", "tp"), None),
            P("tp", "seq"),
            P("seq", None),
            P(("grp", "tp"), "seq"),
            P(("grp", "tp"), "seq"),
        ),
        check_vma=False,
    )
```

time: 722 us -> 170 us (0.24)
  waiting for transfers between devices: 630 us -> 0 us
  Pallas kernels: 0 us -> 147 us
  blocking collectives: 48.8 us -> 0 us
  between operations: 16.4 us -> 2.04 us
  matrix products: 13 us -> 0 us
  local copies, waits for them, and re-layouts: 7.7 us -> 20.1 us
    psum x2 -> x0, waiting for transfers between devices: 429 us -> none  [the longest x1 250 us: shards(): grad_head = lax.psum(head_local, ('grp', 'tp'))]
    pallas_call x0 -> x1, Pallas kernels: none -> 147 us  [shards(): pl.pallas_call(kernel, out_shape=(jax.ShapeDtypeStruct((TOK, 64), F32), j...]
    all_gather x3 -> x0, waiting for transfers between devices: 131 us -> none  [the longest x1 59.5 us: shards(): lax.all_gather(signal, 'tp', axis=0, tiled=True)]
    reduce_scatter x1 -> x0, waiting for transfers between devices: 68.1 us -> none  [shards(): lax.psum_scatter(jnp.concatenate([term_big, term_guide], axis=1).astype(j...]
    psum x3 -> x0, blocking collectives: 48.8 us -> none  [the longest x1 23.9 us: shards(): lax.psum(product_guide.astype(jnp.bfloat16), 'seq').astype(jnp.float32)]
    dot_general x10 -> x0, matrix products: 13 us -> none  [the longest x1 4.37 us: shards(): lax.dot_general(full_big, lax.all_gather(signal, 'tp', axis=0, tiled=True...]
    unnamed x29 -> x19, local copies, waits for them, and re-layouts: 7.55 us -> 15.3 us
  transfers between devices with their start and end apart: 6 -> 0, of which waited for: 6 -> 0; matrix products, arithmetic and copies ran while one was open for 2% -> 0% of each run, Pallas kernels for 0% -> 0%
where the time goes in v1:
time: 170 us
  Pallas kernels  147 us (86%)
  local copies, waits for them, and re-layouts  20.1 us (12%)
  between operations  2.04 us (1%)
    pallas_call x1, Pallas kernels, shards(): pl.pallas_call(kernel, out_shape=(jax.ShapeDtypeStruct((TOK, 64), F32), j...  147 us
    unnamed x19, local copies, waits for them, and re-layouts  15.3 us
    pallas_call x3, local copies, waits for them, and re-layouts, shards(): pl.pallas_call(kernel, out_shape=(jax.ShapeDtypeStruct((TOK, 64), F32), j...  4.89 us

profile of v1, /device:TPU:24, one launch (start us, length us, event | category | flops | bytes accessed | tf_op | source)
XLA Modules:
  0.0 169.6 jit_solution(1709341644819206699)
XLA Ops:
  0.6 0.0 copy-start
  0.6 0.0 copy-start.1
  0.7 0.0 copy-start.2
  2.0 1.5 copy.25.head_g
  3.5 1.5 copy.21.res_g
  5.0 1.5 copy.22.cot_ref
  6.5 1.7 %copy.20.fc_g = bf16[128,560]{1,0:T(8,128)(2,1)} copy(bf16[128,560]{0,1:T(8,128)(2,1)} %param.15) | data formatting | bytes 286720 | tf_op args[1]
  8.2 1.7 copy.24.head_b
  9.9 1.7 copy.27.mod_g
  11.6 0.0 copy-done.2
  11.6 0.8 copy.19.fc_b
  12.5 0.0 copy-done.1
  12.5 0.9 copy.23.proj_g_hbm
  13.3 0.0 copy-done
  13.3 0.9 copy.26.mod_b
  14.3 147.4 %shard_map.173 = (f32[128,64]{1,0:T(8,128)}, bf16[864,640]{1,0:T(8,128)(2,1)}, f32[640,64]{1,0:T(8,128)}, bf16[128,640]{1,0:T(8,128)(2,1)}, bf16[128,192]{1,0:T(8,128)(2,1)}) custom-call(s32[1]{0:T(128)S(6)} %copy.33.time_ref, s32[1]{0:T(128)S(6)} %copy.34.level_ref, f32[8]{0:T(128)} %table_ref.1, bf16[128,864]{1,0:T(8,128)(2,1)} %copy.19.fc_b, ...), custom_call_target="tpu_custom_call" | custom-call | tf_op jit(solution)/shard_map/pallas_call | solution.py:661
  161.6 1.5 copy.28
  163.2 1.6 copy.30
  164.7 1.8 %copy.29 = f32[640,64]{0,1:T(8,128)} copy(f32[640,64]{1,0:T(8,128)} %get-tuple-element.7) | data formatting | bytes 327680 | tf_op jit(solution)/shard_map/pallas_call | solution.py:661
  166.5 0.0 copy-start.3
  166.5 2.4 %copy.35 = bf16[864,640]{1,0:T(8,128)(2,1)} copy(bf16[864,640]{1,0:T(8,128)(2,1)} %get-tuple-element.16) | data formatting | bytes 2211840
  168.9 0.0 copy-done.3
  168.9 0.7 copy.36
Async XLA Ops:
  0.6 12.7 %copy-start = (f32[50,3,640]{2,0,1:T(8,128)S(1)}, f32[50,3,640]{2,0,1:T(8,128)}, u32[]{:S(2)}) copy-start(f32[50,3,640]{2,0,1:T(8,128)} %param.23) | copy-start | bytes 1152004
  0.6 11.8 %copy-start.1 = (bf16[560,192]{0,1:T(8,128)(2,1)S(1)}, bf16[560,192]{0,1:T(8,128)(2,1)}, u32[]{:S(2)}) copy-start(bf16[560,192]{0,1:T(8,128)(2,1)} %param.20) | copy-start | bytes 645124
  0.7 10.9 %copy-start.2 = (bf16[128,864]{0,1:T(8,128)(2,1)S(1)}, bf16[128,864]{0,1:T(8,128)(2,1)}, u32[]{:S(2)}) copy-start(bf16[128,864]{0,1:T(8,128)(2,1)} %param.14) | copy-start | bytes 663556
  166.5 2.4 %copy-start.3 = (bf16[128,640]{1,0:T(8,128)(2,1)S(1)}, bf16[128,640]{1,0:T(8,128)(2,1)}, u32[]{:S(2)}) copy-start(bf16[128,640]{1,0:T(8,128)(2,1)} %get-tuple-element.18) | copy-start | bytes 491524

commit v2 on v0

v2 whole, which is shorter than its diff:
```python
import jax
import jax.numpy as jnp
from jax import lax
from jax.experimental import pallas as pl
from jax.experimental.pallas import tpu as pltpu
from jax.sharding import PartitionSpec as P

MESH = pl.DeviceIdType.MESH
F32 = jnp.float32
BF16 = jnp.bfloat16

DB = 5120
DG = 1536
EPSILON = 1e-06

TOK = 128
WB = 640
WG = 192
HB = 864
HBP = 896
HG = 560
HGP = 640
PATCH = 64
STEPS = 50
NQ = 5
SUB = WB // NQ
UNITS = 8 * NQ
SKEW = 6
GSTEP = 2
NC = 5
SHARD = 224


def remote(src, dst, send, recv, device):
    return pltpu.make_async_remote_copy(
        src_ref=src, dst_ref=dst, send_sem=send, recv_sem=recv, device_id=device, device_id_type=MESH
    )


def kernel(
    time_ref,
    level_ref,
    table_ref,
    fc_b,
    fc_g,
    res_b_in,
    res_g_in,
    cot_in,
    proj_b_in,
    proj_g_in,
    head_b_in,
    head_g_in,
    mod_b_in,
    mod_g_in,
    guided_ref,
    grad_proj_ref,
    grad_head_ref,
    grad_res_b,
    grad_res_g,
    res_b,
    res_g,
    cot_ref,
    proj_b,
    proj_g,
    head_b,
    head_g,
    mod_b,
    mod_g,
    proj_bt,
    proj_gp,
    head_bt,
    gate_b,
    shift_b,
    scale_b,
    gate_g,
    shift_g,
    scale_g,
    fc_all,
    fcg_all,
    term,
    term_g,
    got,
    put,
    cross,
    means,
    gotg_r,
    gotg_l,
    putg_r,
    putg_l,
    dev_b,
    dev_g,
    scaled_b,
    scaled_g,
    spread,
    cots,
    stats,
    stats_g,
    facts,
    signal,
    head_sum,
    parts,
    grad,
    ones,
    zed,
    zed_in,
    final,
    heads,
    made_b,
    in_sem,
    fc_send,
    fc_recv,
    fcg_send,
    fcg_recv,
    cot_send,
    cot_recv,
    mn_send,
    mn_recv,
    in_send,
    in_recv,
    cross_recv,
    out_send,
    out_recv,
    rg_send,
    rg_recv,
    lg_send,
    lg_recv,
    st_send,
    st_recv,
    sg_send,
    sg_recv,
    pt_send,
    pt_recv,
    one_send,
    one_recv,
    z_send,
    z_recv,
    g1_send,
    g1_recv,
    hd_send,
    hd_recv,
):
    grp = lax.axis_index("grp")
    me = lax.axis_index("seq")
    j = lax.axis_index("tp")
    y = lax.rem(grp, 4)
    zh4 = grp - y
    x = lax.div(me, 2)
    core = lax.rem(me, 2)
    sib = me + 1 - 2 * core
    xr = lax.rem(x + 1, 4)
    xl = lax.rem(x + 3, 4)
    xf = lax.rem(x + 2, 4)
    dev_z = {"grp": lax.rem(grp + 4, 8)}

    def seq_peer(n):
        return lax.rem(me + n, 8)

    def tp_peer(n):
        return lax.rem(j + n, 8)

    barrier = pltpu.get_barrier_semaphore()
    for n in range(1, 8):
        pl.semaphore_signal(barrier, inc=1, device_id={"seq": seq_peer(n)}, device_id_type=MESH)
        pl.semaphore_signal(barrier, inc=1, device_id={"tp": tp_peer(n)}, device_id_type=MESH)
    for n in range(1, 4):
        device = {"grp": zh4 + lax.rem(y + n, 4)}
        pl.semaphore_signal(barrier, inc=1, device_id=device, device_id_type=MESH)
    pl.semaphore_signal(barrier, inc=1, device_id=dev_z, device_id_type=MESH)

    loads = {}
    for n, (name, src, dst) in enumerate(
        (
            ("cot", cot_in, cot_ref),
            ("proj_b", proj_b_in, proj_b.at[pl.ds(0, HB)]),
            ("fc", fc_b, fc_all.at[me, pl.ds(0, HB)]),
            ("head_b", head_b_in, head_b),
            ("mod_b", mod_b_in, mod_b),
            ("res_b", res_b_in, res_b),
            ("fcg", fc_g, fcg_all.at[me, pl.ds(0, HG)]),
            ("proj_g", proj_g_in, proj_g),
            ("head_g", head_g_in, head_g),
            ("mod_g", mod_g_in, mod_g),
            ("res_g", res_g_in, res_g),
        )
    ):
        loads[name] = pltpu.make_async_copy(src, dst, in_sem.at[n])
        loads[name].start()

    strength = table_ref[level_ref[0]]
    when = time_ref[0]
    pl.semaphore_wait(barrier, 18)

    def half(h):
        return pl.ds(h * (HB // 2), HB // 2)

    def hidden(s, h):
        return fc_all.at[s, half(h)]

    def seven(ref, send, recv):
        part = ref.at[pl.ds(0, 7)]
        return remote(part, part, send, recv, {"seq": sib})

    def hidden_copy(s, h, k, target, src=None):
        return remote(
            hidden(s, h) if src is None else src.at[half(h)], hidden(s, h), fc_send, fc_recv.at[s, h], {"seq": target}
        )

    to_r, to_l = 2 * xr + core, 2 * xl + core

    def go(copy):
        copy.start()

    def send_hidden(s, h, k, target, src=None):
        go(hidden_copy(s, h, k, target, src))

    def wait_hidden(s, h):
        hidden_copy(s, h, 0, sib).wait_recv()

    send_hidden(me, 0, 0, to_r, fc_b)
    send_hidden(me, 1, 1, to_l, fc_b)
    send_hidden(me, 0, 2, sib, fc_b)
    send_hidden(me, 1, 3, sib, fc_b)
    send_hidden(me, 1, 4, to_r, fc_b)
    send_hidden(me, 0, 5, to_l, fc_b)

    loads["cot"].wait()
    cot = cot_ref[...]
    cots[j] = (strength * cot).astype(BF16)
    for n in range(1, 8):
        go(remote(cots.at[j], cots.at[j], cot_send, cot_recv, {"tp": tp_peer(n)}))

    def pad_rows(value, rows):
        return jnp.concatenate([value, jnp.zeros((rows - value.shape[0], value.shape[1]), value.dtype)], axis=0)

    def pad_lanes(value, lanes):
        return jnp.concatenate([value, jnp.zeros((value.shape[0], lanes - value.shape[1]), value.dtype)], axis=1)

    for s in range(8):
        fc_all[s, HB:HBP, :] = jnp.zeros((HBP - HB, TOK), BF16)
        fcg_all[s, HG:HGP, :] = jnp.zeros((HGP - HG, TOK), BF16)
    proj_b[HB:HBP, :] = jnp.zeros((HBP - HB, WB), BF16)
    loads["mod_b"].wait()
    mods = pad_rows(
        jnp.concatenate([mod_b[n, pl.ds(when, 1), :] for n in range(3)], axis=0), 128
    )
    loads["res_b"].wait()
    for q in range(NC):
        turned = mods[:, 128 * q : 128 * q + 128].T
        at = slice(128 * q, 128 * q + 128)
        gate_b[at, :] = jnp.broadcast_to(turned[:, 0:1], (128, 128))
        shift_b[at, :] = jnp.broadcast_to(turned[:, 1:2], (128, 128))
        scale_b[at, :] = jnp.broadcast_to(1.0 + turned[:, 2:3], (128, 128))
        dev_b[at, :] = res_b[:, at].astype(F32).T
    mean = jnp.sum(dev_b[...], axis=0, keepdims=True) * (1.0 / WB)
    dev_b[...] -= mean
    means[j] = jnp.broadcast_to(mean, (8, TOK))
    for n in range(1, 8):
        go(remote(means.at[j], means.at[j], mn_send, mn_recv, {"tp": tp_peer(n)}))
    loads["proj_b"].wait()
    for q in range(NC):
        proj_bt[128 * q : 128 * q + 128, :] = proj_b[:, 128 * q : 128 * q + 128].T
    loads["fc"].wait()

    def terms(first, second):
        def one(i, carry):
            s = jnp.where(i == 0, first, second)
            term[s] = gate_b[...] * jnp.dot(proj_bt[...], fc_all[s], preferred_element_type=F32)

            @pl.when(s == j)
            def _():
                term[s] += dev_b[...]

            return carry

        lax.fori_loop(0, 2, one, 0)

    left, right, far = to_l, to_r, 2 * xf + core
    left_s, right_s, far_s = 2 * xl + 1 - core, 2 * xr + 1 - core, 2 * xf + 1 - core

    pairs = (
        x,
        1 - lax.rem(x, 2),
        jnp.where(x < 2, 2, x - 2),
        jnp.where(x == 3, 2, 3),
    )

    def block_at(b):
        n = lax.div(b, 2)
        pair = jnp.where(n == 0, pairs[0], jnp.where(n == 1, pairs[1], jnp.where(n == 2, pairs[2], pairs[3])))
        return 2 * pair + jnp.where(lax.rem(b, 2) == 0, core, 1 - core)

    def place_of(d):
        return sum(jnp.where(block_at(jnp.int32(b)) == d, b, 0) for b in range(8))

    wait_hidden(sib, 0)
    wait_hidden(sib, 1)
    terms(me, sib)

    def fcg_copy(s, n, target, src):
        return remote(src, fcg_all.at[s, pl.ds(0, HG)], fcg_send, fcg_recv.at[s], {"seq": target})

    relays = (
        (left, 0, 6, to_r),
        (left, 0, 7, sib),
        (right, 1, 8, to_l),
        (right, 1, 9, sib),
        (left, 1, 10, sib),
        (right, 0, 11, sib),
        (far, 0, 12, sib),
        (far, 1, 13, sib),
    )

    def relay(n):
        s, h, k, target = relays[n]
        hidden_copy(s, h, k, target).start()

    def scale_all():
        def one(d, carry):
            scaled_b[d] = (
                jnp.dot(head_bt[...], pad_rows(cots[d], 128), preferred_element_type=F32) * scale_b[...]
            )
            return carry

        lax.fori_loop(0, 8, one, 0)

    def near():
        wait_hidden(left, 0)
        relay(0)
        relay(1)
        wait_hidden(right, 1)
        relay(2)
        relay(3)
        wait_hidden(left, 1)
        relay(4)
        wait_hidden(right, 0)
        relay(5)
        for h in range(2):
            wait_hidden(left_s, h)
            wait_hidden(right_s, h)
        terms(2 * pairs[1], 2 * pairs[1] + 1)
        scale_all()

    def opposite():
        wait_hidden(far, 0)
        relay(6)
        wait_hidden(far, 1)
        relay(7)
        wait_hidden(far_s, 0)
        wait_hidden(far_s, 1)
        terms(2 * pairs[2], 2 * pairs[2] + 1)
        for n in range(1, 8):
            fcg_copy(me, n, seq_peer(n), fc_g).start()

    def rest():
        terms(2 * pairs[3], 2 * pairs[3] + 1)

    in_left = j < 4
    place = jnp.where(in_left, j, 7 - j)
    toward = {"tp": jnp.where(in_left, j + 1, j - 1)}
    away = {"tp": jnp.where(in_left, j - 1, j + 1)}

    def piece(q):
        return pl.ds(pl.multiple_of(q * SUB, 16), SUB)

    def in_copy(b, q):
        return remote(put.at[b, piece(q)], got.at[b, piece(q)], in_send, in_recv.at[b, q], toward)

    def cross_copy(b, q):
        return remote(put.at[b, piece(q)], cross.at[b, piece(q)], in_send, cross_recv.at[b, q], toward)

    def out_copy(b, q):
        ref = spread.at[b, piece(q)]
        return remote(ref, ref, out_send, out_recv.at[b, q], away)

    def stat_copy(s, n, d, target):
        ref = stats.at[d, s]
        return remote(ref, ref, st_send, st_recv.at[d], {"seq": target})

    def block_stats(d, b):
        up = scaled_b[d]
        value = spread[b].astype(F32)
        mean = jnp.sum(value, axis=0, keepdims=True) * (1.0 / WB)
        value -= mean
        stats[d, me] = pad_rows(
            jnp.concatenate(
                [
                    means[d, 0:1] + mean,
                    jnp.sum(value * value, axis=0, keepdims=True),
                    jnp.sum(up, axis=0, keepdims=True),
                    jnp.sum(up * value, axis=0, keepdims=True),
                ],
                axis=0,
            ),
            8,
        )
        for n in range(1, 8):
            stat_copy(me, n, d, seq_peer(n)).start()

    def norm(every, mine, width, whole):
        centre = sum(r[0:1] for r in every) * (1.0 / 8)
        gaps = [r[0:1] - centre for r in every]
        square_sum = sum(r[1:2] + width * (g * g) for r, g in zip(every, gaps))
        inverse = lax.rsqrt(square_sum * (1.0 / whole) + EPSILON)
        first = sum(r[2:3] for r in every) * (1.0 / whole)
        cross_sum = sum(r[3:4] + r[2:3] * g for r, g in zip(every, gaps))
        second = inverse * cross_sum * (1.0 / whole)
        offset = inverse * (mine - centre)
        return inverse, offset, inverse * inverse * second, inverse * (first + offset * second)

    def consume(d):
        d = jnp.int32(d)
        b = place_of(d)
        seven(stats.at[d], st_send, st_recv.at[d]).wait_recv()
        every = [stats[d, s] for s in range(8)]
        inverse, offset, slope, base = norm(every, means[d, 0:1], float(WB), float(DB))
        facts[d] = pad_rows(jnp.concatenate([inverse, offset, slope, base], axis=0), 8)
        value = spread[b].astype(F32)
        signal[d] = (
            gate_b[...] * (inverse * scaled_b[d] - slope * value - base)
        ).astype(BF16)
        shaped = ((inverse * value + offset) * scale_b[...] + shift_b[...]).astype(BF16)
        head_sum[...] += lax.dot_general(
            cots[d], shaped, (((1,), (1,)), ((), ())), preferred_element_type=F32
        )

    def guide_copy(right_way, i):
        if right_way:
            return remote(putg_r.at[i], gotg_r.at[i], rg_send.at[i], rg_recv.at[i], {"tp": j + 1})
        return remote(putg_l.at[i], gotg_l.at[i], lg_send.at[i], lg_recv.at[i], {"tp": j - 1})

    def guide_term(s):
        @pl.when(s != me)
        def _():
            fcg_copy(s, 0, s, fcg_all.at[s, pl.ds(0, HG)]).wait_recv()

        return jnp.dot(proj_gp[...], fcg_all[s], preferred_element_type=F32)

    def guide_step(t):
        for right_way in (True, False):
            far_end = j if right_way else 7 - j
            w = t - UNITS - SKEW * far_end
            i = lax.div(w, GSTEP)
            put, got = (putg_r, gotg_r) if right_way else (putg_l, gotg_l)

            @pl.when((w >= 0) & (lax.rem(w, GSTEP) == 0) & (i < 7 - far_end))
            def _():
                own = guide_term(7 - i if right_way else i)

                @pl.when(far_end > 0)
                def _():
                    guide_copy(right_way, i).wait_recv()
                    put[i] = (got[i].astype(F32) + own).astype(BF16)

                @pl.when(far_end == 0)
                def _():
                    put[i] = own.astype(BF16)

                guide_copy(right_way, i).start()

    def tick(t, carry):
        for at, action in ((2, near), (4, opposite), (6, rest)):
            pl.when(t == at * NQ)(action)
        u = t - SKEW * place

        @pl.when((u >= 0) & (u < UNITS))
        def _():
            b = lax.div(u, NQ)
            q = lax.rem(u, NQ)
            own = term[block_at(b), piece(q), :]

            @pl.when(place > 0)
            def _():
                in_copy(b, q).wait_recv()
                put[b, piece(q), :] = (got[b, piece(q), :].astype(F32) + own).astype(BF16)

            @pl.when(place == 0)
            def _():
                put[b, piece(q), :] = own.astype(BF16)

            @pl.when(place < 3)
            def _():
                in_copy(b, q).start()

            @pl.when(place == 3)
            def _():
                cross_copy(b, q).start()

        v = t - SKEW * (7 - place)

        @pl.when((v >= 0) & (v < UNITS))
        def _():
            b = lax.div(v, NQ)
            q = lax.rem(v, NQ)

            @pl.when(place == 3)
            def _():
                cross_copy(b, q).wait_recv()
                spread[b, piece(q), :] = add(put[b, piece(q), :], cross[b, piece(q), :])

            @pl.when(place < 3)
            def _():
                out_copy(b, q).wait_recv()

            @pl.when(place > 0)
            def _():
                out_copy(b, q).start()

            for d, (at_b, at_q) in enumerate(((6, 3), (7, 0), (7, 1), (7, 2))):

                @pl.when((b == at_b) & (q == at_q))
                def _():
                    consume(d)

            @pl.when(q == NQ - 1)
            def _():
                block_stats(block_at(b), b)

        guide_step(t)
        return carry

    def add(a, b):
        return (a.astype(F32) + b.astype(F32)).astype(BF16)

    loads["head_b"].wait()
    head_bt[...] = pad_lanes(head_b[...].T, 128)
    loads["proj_g"].wait()
    proj_gp[...] = pad_lanes(proj_g[...], HGP)
    loads["fcg"].wait()
    head_sum[...] = jnp.zeros_like(head_sum)
    seven(cots, cot_send, cot_recv).wait_recv()
    seven(means, mn_send, mn_recv).wait_recv()

    lax.fori_loop(0, UNITS + 7 * SKEW, tick, 0)
    for d in range(4, 8):
        consume(d)

    def rows(shard):
        return pl.ds(pl.multiple_of(shard * SHARD, 16), SHARD)

    def y_peer(n):
        return lax.rem(y + n, 4)

    def one_copy(c, n):
        p = y_peer(n)
        return remote(grad.at[c, rows(p)], ones.at[c, n - 1], one_send, one_recv.at[c], {"grp": zh4 + p})

    def z_copy(c):
        return remote(zed.at[c], zed_in.at[c], z_send, z_recv.at[c], dev_z)

    def back_copy(c, n):
        ref = final.at[c, rows(y)]
        return remote(ref, ref, g1_send, g1_recv.at[c], {"grp": zh4 + y_peer(n)})

    def three(c, send, recv):
        part = final.at[c, pl.ds(0, 3 * SHARD)]
        return remote(part, part, send, recv, dev_z)

    patch_rows = head_sum[pl.ds(pl.multiple_of(j * 8, 8), 8), :]
    spare = [patch_rows[:, 128 * q : 128 * q + 128] for q in range(NC)]
    spare = [
        jnp.concatenate(spare[0:4], axis=0),
        pad_rows(spare[4], 32),
    ] + [jnp.zeros((32, 128), F32)] * 3
    def guide_stats():
        loads["head_g"].wait()
        loads["mod_g"].wait()
        loads["res_g"].wait()
        mods = jnp.concatenate([mod_g[n, pl.ds(when, 1), :] for n in range(3)], axis=0)
        mods = pad_rows(pad_lanes(mods, 256), 128)
        for q in range(2):
            high = min(128, WG - 128 * q)
            turned = mods[:, 128 * q : 128 * q + 128].T[0:high]
            at = slice(128 * q, 128 * q + high)
            gate_g[at, :] = jnp.broadcast_to(turned[:, 0:1], (high, 128))
            shift_g[at, :] = jnp.broadcast_to(turned[:, 1:2], (high, 128))
            scale_g[at, :] = jnp.broadcast_to(1.0 + turned[:, 2:3], (high, 128))
        cot_g = ((1.0 - strength) * cot_ref[...]).astype(BF16)
        scaled_g[...] = (
            lax.dot_general(head_g[...], cot_g, (((0,), (0,)), ((), ())), preferred_element_type=F32)
            * scale_g[...]
        )
        term_g[...] = guide_term(j)
        for right_way in (True, False):
            place = j if right_way else 7 - j
            got = gotg_r if right_way else gotg_l

            @pl.when(place > 0)
            def _():
                guide_copy(right_way, 7 - place).wait_recv()
                term_g[...] += got[7 - place].astype(F32)

        stream = res_g[...].astype(F32) + gate_g[...] * term_g[...]
        mean_g = jnp.sum(stream, axis=0, keepdims=True) * (1.0 / WG)
        away_g = stream - mean_g
        dev_g[...] = away_g
        up_g = scaled_g[...]
        stats_g[me] = pad_rows(
            jnp.concatenate(
                [
                    mean_g,
                    jnp.sum(away_g * away_g, axis=0, keepdims=True),
                    jnp.sum(up_g, axis=0, keepdims=True),
                    jnp.sum(up_g * away_g, axis=0, keepdims=True),
                ],
                axis=0,
            ),
            8,
        )
        for n in range(1, 8):
            go(remote(stats_g.at[me], stats_g.at[me], sg_send, sg_recv, {"seq": seq_peer(n)}))

    own_at = place_of(j)

    def own_big():
        inverse, offset, slope, base = (facts[j, n : n + 1, :] for n in range(4))
        value = spread[own_at].astype(F32)
        own = inverse * scaled_b[j] - slope * value - base
        for q in range(NC):
            grad_res_b[:, 128 * q : 128 * q + 128] = own[128 * q : 128 * q + 128, :].T.astype(BF16)
        shaped = ((inverse * value + offset) * scale_b[...] + shift_b[...]).astype(BF16)
        made_b[...] = strength * jnp.dot(head_b[...], shaped, preferred_element_type=F32)
    def own_guide():
        seven(stats_g, sg_send, sg_recv).wait_recv()
        inverse, offset, slope, base = norm([stats_g[s] for s in range(8)], stats_g[me][0:1], float(WG), float(DG))
        grad_res_g[...] = (inverse * scaled_g[...] - slope * dev_g[...] - base).astype(BF16)
        shaped = ((inverse * dev_g[...] + offset) * scale_g[...] + shift_g[...]).astype(BF16)
        out_g = jnp.dot(head_g[...], shaped, preferred_element_type=F32)
        parts[me] = (made_b[...] + (1.0 - strength) * out_g).astype(BF16)
        for n in range(1, 8):
            go(remote(parts.at[me], parts.at[me], pt_send, pt_recv, {"seq": seq_peer(n)}))

    def settle():
        part = fc_all.at[pl.ds(0, 7), pl.ds(0, HB)]
        remote(part, part, fc_send, fc_recv.at[0, 0], {"seq": sib}).wait_send()
        part = fcg_all.at[pl.ds(0, 7), pl.ds(0, HG)]
        remote(part, part, fcg_send, fcg_recv.at[0], {"seq": sib}).wait_send()
        seven(cots, cot_send, cot_recv).wait_send()
        seven(means, mn_send, mn_recv).wait_send()
        remote(put, got, in_send, in_recv.at[0, 0], {"seq": sib}).wait_send()

        @pl.when(place > 0)
        def _():
            remote(spread, spread, out_send, out_recv.at[0, 0], {"seq": sib}).wait_send()

        part = scaled_b.at[0, pl.ds(0, 7 * 8 * 8)]
        remote(part, part, st_send, st_recv.at[0], {"seq": sib}).wait_send()

        def drain(b, carry):
            for right_way in (True, False):

                @pl.when(b < (7 - j if right_way else j))
                def _():
                    guide_copy(right_way, b).wait_send()

            return carry

        lax.fori_loop(0, 7, drain, 0)

    def stage_grad(c):
        at = slice(128 * c, 128 * c + 128)
        grad[c, 0:HB, :] = lax.dot_general(
            jnp.concatenate([fc_all[s, 0:HB, :] for s in range(8)], axis=1),
            jnp.concatenate([signal[s, at, :] for s in range(8)], axis=1),
            (((1,), (1,)), ((), ())),
            preferred_element_type=F32,
        ).astype(BF16)
        grad[c, HB:HBP, :] = spare[c].astype(BF16)
        for n in (1, 3, 2):
            go(one_copy(c, n))

    def stage_one(c):
        three(c, one_send, one_recv.at[c]).wait_recv()
        total = grad[c, rows(y), :].astype(F32)
        for n in range(3):
            total += ones[c, n].astype(F32)
        zed[c] = total.astype(BF16)
        go(z_copy(c))

    def stage_z(c):
        z_copy(c).wait_recv()
        final[c, rows(y), :] = add(zed[c], zed_in[c])
        for n in (2, 1, 3):
            go(back_copy(c, n))

    def stage_out(c):
        three(c, g1_send, g1_recv.at[c]).wait_recv()
        grad_proj_ref[:, 128 * c : 128 * c + 128] = final[c, 0:HB, :]
        if c == 1:
            heads[j, 0:32, :] = final[0, HB:HBP, :]
            heads[j, 32:64, :] = final[1, HB:HBP, :]
            for n in range(1, 8):
                go(remote(heads.at[j], heads.at[j], hd_send, hd_recv, {"tp": tp_peer(n)}))

    def predict():
        seven(parts, pt_send, pt_recv).wait_recv()
        guided_ref[...] = sum(parts[s].astype(F32) for s in range(8))

    def collect_heads():
        seven(heads, hd_send, hd_recv).wait_recv()
        for p in range(8):
            block = heads[p].astype(F32)
            for q in range(NC):
                grad_head_ref[8 * p : 8 * p + 8, 128 * q : 128 * q + 128] = block[8 * q : 8 * q + 8]

    A, B, C, D = stage_grad, stage_one, stage_z, stage_out
    for stage, c in ((A, 0), (A, 1), (B, 0), (A, 2), (B, 1), (A, 3), (A, 4), (B, 2), (B, 3)):
        stage(c)
    guide_stats()
    for stage, c in ((B, 4), (C, 0)):
        stage(c)
    own_big()
    own_guide()
    C(1)
    D(0)
    settle()
    C(2)
    D(1)
    predict()
    C(3)
    D(2)
    collect_heads()
    C(4)
    D(3)
    D(4)

    whole = final.at[:, pl.ds(0, 3 * SHARD)]
    remote(whole, whole, one_send, one_recv.at[0], dev_z).wait_send()
    remote(zed, zed_in, z_send, z_recv.at[0], dev_z).wait_send()
    remote(whole, whole, g1_send, g1_recv.at[0], dev_z).wait_send()
    seven(stats_g, sg_send, sg_recv).wait_send()
    seven(parts, pt_send, pt_recv).wait_send()
    seven(heads, hd_send, hd_recv).wait_send()


def shards(
    fc_big,
    fc_guide,
    res_big,
    res_guide,
    cotangent,
    proj_big,
    proj_guide,
    head_big,
    head_guide,
    modulation_big,
    modulation_guide,
    weight_table,
    time_index,
    weight_index,
):
    smem = pl.BlockSpec(memory_space=pltpu.SMEM)
    vmem = pl.BlockSpec(memory_space=pltpu.VMEM)
    hbm = pl.BlockSpec(memory_space=pl.ANY)
    dma = pltpu.SemaphoreType.DMA
    V = pltpu.VMEM
    shapes = (
        ((PATCH, TOK), F32),
        ((HB, WB), BF16),
        ((PATCH, WB), F32),
        ((TOK, WB), BF16),
        ((WG, TOK), BF16),
    )
    made = pl.pallas_call(
        kernel,
        out_shape=tuple(V(*s) for s in shapes),
        in_specs=[smem] * 3 + [hbm] * 11,
        out_specs=(vmem,) * 5,
        scratch_shapes=[
            V((TOK, WB), BF16),
            V((WG, TOK), BF16),
            V((PATCH, TOK), F32),
            V((HBP, WB), BF16),
            V((WG, HG), BF16),
            V((PATCH, WB), BF16),
            V((PATCH, WG), BF16),
            V((3, STEPS, WB), F32),
            V((3, STEPS, WG), F32),
            V((WB, HBP), BF16),
            V((WG, HGP), BF16),
            V((WB, 128), BF16),
            V((WB, 128), F32),
            V((WB, 128), F32),
            V((WB, 128), F32),
            V((WG, 128), F32),
            V((WG, 128), F32),
            V((WG, 128), F32),
            V((8, HBP, TOK), BF16),
            V((8, HGP, TOK), BF16),
            V((8, WB, TOK), F32),
            V((WG, TOK), F32),
            V((8, WB, TOK), BF16),
            V((8, WB, TOK), BF16),
            V((8, WB, TOK), BF16),
            V((8, 8, TOK), F32),
            V((7, WG, TOK), BF16),
            V((7, WG, TOK), BF16),
            V((7, WG, TOK), BF16),
            V((7, WG, TOK), BF16),
            V((WB, TOK), F32),
            V((WG, TOK), F32),
            V((8, WB, TOK), F32),
            V((WG, TOK), F32),
            V((8, WB, TOK), BF16),
            V((8, PATCH, TOK), BF16),
            V((8, 8, 8, TOK), F32),
            V((8, 8, TOK), F32),
            V((8, 8, TOK), F32),
            V((8, WB, TOK), BF16),
            V((PATCH, WB), F32),
            V((8, PATCH, TOK), BF16),
            V((NC, HBP, 128), BF16),
            V((NC, 3, SHARD, 128), BF16),
            V((NC, SHARD, 128), BF16),
            V((NC, SHARD, 128), BF16),
            V((NC, HBP, 128), BF16),
            V((8, 64, 128), BF16),
            V((PATCH, TOK), F32),
            dma((11,)),
            dma(()),
            dma((8, 2)),
            dma(()),
            dma((8,)),
            dma(()),
            dma(()),
            dma(()),
            dma(()),
            dma(()),
            dma((8, NQ)),
            dma((8, NQ)),
            dma(()),
            dma((8, NQ)),
            dma((7,)),
            dma((7,)),
            dma((7,)),
            dma((7,)),
            dma(()),
            dma((8,)),
            dma(()),
            dma(()),
            dma(()),
            dma(()),
            dma(()),
            dma((NC,)),
            dma(()),
            dma((NC,)),
            dma(()),
            dma((NC,)),
            dma(()),
            dma(()),
        ],
        compiler_params=pltpu.CompilerParams(
            collective_id=0, has_side_effects=True, vmem_limit_bytes=56 * 2**20
        ),
    )(
        time_index,
        weight_index,
        weight_table,
        fc_big.T,
        fc_guide.T,
        res_big,
        res_guide.T,
        cotangent.T,
        proj_big,
        proj_guide.T,
        head_big.T,
        head_guide.T,
        modulation_big.transpose(1, 0, 2),
        modulation_guide.transpose(1, 0, 2),
    )
    guided, grad_proj, grad_head, grad_res_big, grad_res_guide = made
    return guided.T, grad_proj, grad_head.T, grad_res_big, grad_res_guide.T


def solution(mesh):
    placed = (
        P(("grp", "seq"), "tp"),
        P(("grp", "seq"), "tp"),
        P(("grp", "tp"), "seq"),
        P(("grp", "tp"), "seq"),
        P(("grp", "tp"), None),
        P("tp", "seq"),
        P("tp", "seq"),
        P("seq", None),
        P("seq", None),
        P(None, None, "seq"),
        P(None, None, "seq"),
        P(),
        P("grp"),
        P("grp"),
    )
    return jax.shard_map(
        shards,
        mesh=mesh,
        in_specs=placed,
        out_specs=(
            P(("grp", "tp"), None),
            P("tp", "seq"),
            P("seq", None),
            P(("grp", "tp"), "seq"),
            P(("grp", "tp"), "seq"),
        ),
        check_vma=False,
    )
```

time: 722 us -> 139 us (0.19)
  waiting for transfers between devices: 630 us -> 0 us
  Pallas kernels: 0 us -> 132 us
  blocking collectives: 48.8 us -> 0 us
  between operations: 16.4 us -> 1.94 us
  matrix products: 13 us -> 0 us
    psum x2 -> x0, waiting for transfers between devices: 429 us -> none  [the longest x1 250 us: shards(): grad_head = lax.psum(head_local, ('grp', 'tp'))]
    pallas_call x0 -> x1, Pallas kernels: none -> 132 us  [shards(): pl.pallas_call(kernel, out_shape=tuple((V(*s) for s in shapes)), in_specs...]
    all_gather x3 -> x0, waiting for transfers between devices: 131 us -> none  [the longest x1 59.5 us: shards(): lax.all_gather(signal, 'tp', axis=0, tiled=True)]
    reduce_scatter x1 -> x0, waiting for transfers between devices: 68.1 us -> none  [shards(): lax.psum_scatter(jnp.concatenate([term_big, term_guide], axis=1).astype(j...]
    psum x3 -> x0, blocking collectives: 48.8 us -> none  [the longest x1 23.9 us: shards(): lax.psum(product_guide.astype(jnp.bfloat16), 'seq').astype(jnp.float32)]
    dot_general x10 -> x0, matrix products: 13 us -> none  [the longest x1 4.37 us: shards(): lax.dot_general(full_big, lax.all_gather(signal, 'tp', axis=0, tiled=True...]
  transfers between devices with their start and end apart: 6 -> 0, of which waited for: 6 -> 0; matrix products, arithmetic and copies ran while one was open for 2% -> 0% of each run, Pallas kernels for 0% -> 0%
where the time goes in v2:
time: 139 us; the launch traced here: 138 us
  Pallas kernels  132 us (95%)
  local copies, waits for them, and re-layouts  3.56 us (3%)
  between operations  1.94 us (1%)
    pallas_call x1, Pallas kernels, shards(): pl.pallas_call(kernel, out_shape=tuple((V(*s) for s in shapes)), in_specs...  132 us
    unnamed x5, local copies, waits for them, and re-layouts  3.56 us

profile of v2, /device:TPU:24, one launch (start us, length us, event | category | flops | bytes accessed | tf_op | source)
XLA Modules:
  0.0 137.9 jit_solution(8942023714598812254)
XLA Ops:
  1.9 132.4 %shard_map.173 = (f32[64,128]{1,0:T(8,128)S(1)}, bf16[864,640]{1,0:T(8,128)(2,1)S(1)}, f32[64,640]{1,0:T(8,128)S(1)}, bf16[128,640]{1,0:T(8,128)(2,1)S(1)}, bf16[192,128]{1,0:T(8,128)(2,1)S(1)}) custom-call(s32[1]{0:T(128)S(6)} %copy.29.time_ref, s32[1]{0:T(128)S(6)} %copy.30.level_ref, f32[8]{0:T(128)} %table_ref.1, bf16[864,128]{1,0:T(8,128)(2,1)} %bitcast.17, ...), custom_call_target="tpu_custom_call" | custom-call | tf_op jit(solution)/shard_map/pallas_call | solution.py:763
  134.3 0.6 copy.24
  134.9 0.6 copy.28
  135.6 0.7 copy.26
  136.2 0.7 copy.27
  136.9 1.0 copy.25

commit v3 on v2

--- a/solution.py
+++ b/solution.py
@@ -26,6 +26,7 @@
 SUB = WB // NQ
 UNITS = 8 * NQ
 SKEW = 6
+DEPTH = 3
 GSTEP = 2
 NC = 5
 SHARD = 224
@@ -117,7 +118,6 @@
     mn_recv,
     in_send,
     in_recv,
-    cross_recv,
     out_send,
     out_recv,
     rg_send,
@@ -261,18 +261,12 @@
         proj_bt[128 * q : 128 * q + 128, :] = proj_b[:, 128 * q : 128 * q + 128].T
     loads["fc"].wait()
 
-    def terms(first, second):
-        def one(i, carry):
-            s = jnp.where(i == 0, first, second)
-            term[s] = gate_b[...] * jnp.dot(proj_bt[...], fc_all[s], preferred_element_type=F32)
-
-            @pl.when(s == j)
-            def _():
-                term[s] += dev_b[...]
-
-            return carry
-
-        lax.fori_loop(0, 2, one, 0)
+    def terms(s):
+        term[s] = gate_b[...] * jnp.dot(proj_bt[...], fc_all[s], preferred_element_type=F32)
+
+        @pl.when(s == j)
+        def _():
+            term[s] += dev_b[...]
 
     left, right, far = to_l, to_r, 2 * xf + core
     left_s, right_s, far_s = 2 * xl + 1 - core, 2 * xr + 1 - core, 2 * xf + 1 - core
@@ -292,9 +286,7 @@
     def place_of(d):
         return sum(jnp.where(block_at(jnp.int32(b)) == d, b, 0) for b in range(8))
 
-    wait_hidden(sib, 0)
-    wait_hidden(sib, 1)
-    terms(me, sib)
+    terms(me)
 
     def fcg_copy(s, n, target, src):
         return remote(src, fcg_all.at[s, pl.ds(0, HG)], fcg_send, fcg_recv.at[s], {"seq": target})
@@ -323,6 +315,10 @@
 
         lax.fori_loop(0, 8, one, 0)
 
+    def beside():
+        wait_hidden(sib, 0)
+        wait_hidden(sib, 1)
+
     def near():
         wait_hidden(left, 0)
         relay(0)
@@ -330,29 +326,39 @@
         wait_hidden(right, 1)
         relay(2)
         relay(3)
+
+    def near_rest():
         wait_hidden(left, 1)
         relay(4)
         wait_hidden(right, 0)
         relay(5)
+
+    def near_others():
         for h in range(2):
             wait_hidden(left_s, h)
             wait_hidden(right_s, h)
-        terms(2 * pairs[1], 2 * pairs[1] + 1)
-        scale_all()
 
     def opposite():
         wait_hidden(far, 0)
         relay(6)
         wait_hidden(far, 1)
         relay(7)
+
+    def opposite_others():
         wait_hidden(far_s, 0)
         wait_hidden(far_s, 1)
-        terms(2 * pairs[2], 2 * pairs[2] + 1)
         for n in range(1, 8):
             fcg_copy(me, n, seq_peer(n), fc_g).start()
 
-    def rest():
-        terms(2 * pairs[3], 2 * pairs[3] + 1)
+    events = (
+        (NQ, beside),
+        (2 * NQ - 2, near),
+        (2 * NQ, near_rest),
+        (2 * NQ + 2, scale_all),
+        (3 * NQ, near_others),
+        (4 * NQ - 2, opposite),
+        (5 * NQ, opposite_others),
+    )
 
     in_left = j < 4
     place = jnp.where(in_left, j, 7 - j)
@@ -363,10 +369,10 @@
         return pl.ds(pl.multiple_of(q * SUB, 16), SUB)
 
     def in_copy(b, q):
-        return remote(put.at[b, piece(q)], got.at[b, piece(q)], in_send, in_recv.at[b, q], toward)
+        return remote(put.at[b, piece(q)], got.at[b, piece(q)], in_send.at[lax.rem(b * NQ + q, DEPTH)], in_recv.at[b, q], toward)
 
     def cross_copy(b, q):
-        return remote(put.at[b, piece(q)], cross.at[b, piece(q)], in_send, cross_recv.at[b, q], toward)
+        return remote(put.at[b, piece(q)], cross.at[b, piece(q)], in_send.at[lax.rem(b * NQ + q, DEPTH)], out_recv.at[b, q], toward)
 
     def out_copy(b, q):
         ref = spread.at[b, piece(q)]
@@ -458,8 +464,13 @@
                 guide_copy(right_way, i).start()
 
     def tick(t, carry):
-        for at, action in ((2, near), (4, opposite), (6, rest)):
-            pl.when(t == at * NQ)(action)
+        for at, action in events:
+            pl.when(t == at)(action)
+
+        @pl.when((lax.rem(t, NQ) == 0) & (t > 0) & (t < UNITS))
+        def _():
+            terms(block_at(lax.div(t, NQ)))
+
         u = t - SKEW * place
 
         @pl.when((u >= 0) & (u < UNITS))
@@ -476,6 +487,10 @@
             @pl.when(place == 0)
             def _():
                 put[b, piece(q), :] = own.astype(BF16)
+
+            @pl.when(u >= DEPTH)
+            def _():
+                in_copy(b, q).wait_send()
 
             @pl.when(place < 3)
             def _():
@@ -636,7 +651,8 @@
         remote(part, part, fcg_send, fcg_recv.at[0], {"seq": sib}).wait_send()
         seven(cots, cot_send, cot_recv).wait_send()
         seven(means, mn_send, mn_recv).wait_send()
-        remote(put, got, in_send, in_recv.at[0, 0], {"seq": sib}).wait_send()
+        for u in range(UNITS - DEPTH, UNITS):
+            in_copy(jnp.int32(u // NQ), jnp.int32(u % NQ)).wait_send()
 
         @pl.when(place > 0)
         def _():
@@ -665,7 +681,7 @@
             preferred_element_type=F32,
         ).astype(BF16)
         grad[c, HB:HBP, :] = spare[c].astype(BF16)
-        for n in (1, 3, 2):
+        for n in (2, 1, 3):
             go(one_copy(c, n))
 
     def stage_one(c):
@@ -674,7 +690,6 @@
         for n in range(3):
             total += ones[c, n].astype(F32)
         zed[c] = total.astype(BF16)
-        go(z_copy(c))
 
     def stage_z(c):
         z_copy(c).wait_recv()
@@ -702,15 +717,30 @@
             for q in range(NC):
                 grad_head_ref[8 * p : 8 * p + 8, 128 * q : 128 * q + 128] = block[8 * q : 8 * q + 8]
 
-    A, B, C, D = stage_grad, stage_one, stage_z, stage_out
-    for stage, c in ((A, 0), (A, 1), (B, 0), (A, 2), (B, 1), (A, 3), (A, 4), (B, 2), (B, 3)):
-        stage(c)
+    def stage_across(c):
+        go(z_copy(c))
+
+    A, B, Z, C, D = stage_grad, stage_one, stage_across, stage_z, stage_out
+    A(0)
+    A(1)
+    B(0)
+    Z(0)
+    A(2)
+    B(1)
+    Z(1)
+    A(3)
+    B(2)
+    Z(2)
+    A(4)
+    B(3)
     guide_stats()
-    for stage, c in ((B, 4), (C, 0)):
-        stage(c)
+    B(4)
     own_big()
+    C(0)
+    Z(3)
     own_guide()
     C(1)
+    Z(4)
     D(0)
     settle()
     C(2)
@@ -824,8 +854,7 @@
             dma(()),
             dma(()),
             dma(()),
-            dma(()),
-            dma((8, NQ)),
+            dma((DEPTH,)),
             dma((8, NQ)),
             dma(()),
             dma((8, NQ)),

time: 139 us -> 132 us (0.950)
  Pallas kernels: 132 us -> 126 us
    pallas_call x1, Pallas kernels: 132 us -> 126 us  [shards(): pl.pallas_call(kernel, out_shape=tuple((V(*s) for s in shapes)), in_specs...]
where the time goes in v3:
time: 132 us; the launch traced here: 131 us
  Pallas kernels  126 us (95%)
  local copies, waits for them, and re-layouts  3.56 us (3%)
  between operations  1.94 us (1%)
    pallas_call x1, Pallas kernels, shards(): pl.pallas_call(kernel, out_shape=tuple((V(*s) for s in shapes)), in_specs...  126 us
    unnamed x5, local copies, waits for them, and re-layouts  3.56 us

profile of v3, /device:TPU:24, one launch (start us, length us, event | category | flops | bytes accessed | tf_op | source)
XLA Modules:
  0.0 131.4 jit_solution(304231549348921107)
XLA Ops:
  1.9 125.9 %shard_map.173 = (f32[64,128]{1,0:T(8,128)S(1)}, bf16[864,640]{1,0:T(8,128)(2,1)S(1)}, f32[64,640]{1,0:T(8,128)S(1)}, bf16[128,640]{1,0:T(8,128)(2,1)S(1)}, bf16[192,128]{1,0:T(8,128)(2,1)S(1)}) custom-call(s32[1]{0:T(128)S(6)} %copy.29.time_ref, s32[1]{0:T(128)S(6)} %copy.30.level_ref, f32[8]{0:T(128)} %table_ref.1, bf16[864,128]{1,0:T(8,128)(2,1)} %bitcast.17, ...), custom_call_target="tpu_custom_call" | custom-call | tf_op jit(solution)/shard_map/pallas_call | solution.py:793
  127.9 0.6 copy.24
  128.5 0.6 copy.28
  129.1 0.7 copy.26
  129.8 0.7 copy.27
  130.4 1.0 copy.25

commit v4 on v3

--- a/solution.py
+++ b/solution.py
@@ -25,7 +25,7 @@
 NQ = 5
 SUB = WB // NQ
 UNITS = 8 * NQ
-SKEW = 6
+SKEW = 5
 DEPTH = 3
 GSTEP = 2
 NC = 5
@@ -170,12 +170,12 @@
     loads = {}
     for n, (name, src, dst) in enumerate(
         (
-            ("cot", cot_in, cot_ref),
+            ("mod_b", mod_b_in, mod_b),
+            ("res_b", res_b_in, res_b),
             ("proj_b", proj_b_in, proj_b.at[pl.ds(0, HB)]),
             ("fc", fc_b, fc_all.at[me, pl.ds(0, HB)]),
+            ("cot", cot_in, cot_ref),
             ("head_b", head_b_in, head_b),
-            ("mod_b", mod_b_in, mod_b),
-            ("res_b", res_b_in, res_b),
             ("fcg", fc_g, fcg_all.at[me, pl.ds(0, HG)]),
             ("proj_g", proj_g_in, proj_g),
             ("head_g", head_g_in, head_g),
@@ -223,12 +223,6 @@
     send_hidden(me, 1, 4, to_r, fc_b)
     send_hidden(me, 0, 5, to_l, fc_b)
 
-    loads["cot"].wait()
-    cot = cot_ref[...]
-    cots[j] = (strength * cot).astype(BF16)
-    for n in range(1, 8):
-        go(remote(cots.at[j], cots.at[j], cot_send, cot_recv, {"tp": tp_peer(n)}))
-
     def pad_rows(value, rows):
         return jnp.concatenate([value, jnp.zeros((rows - value.shape[0], value.shape[1]), value.dtype)], axis=0)
 
@@ -237,7 +231,6 @@
 
     for s in range(8):
         fc_all[s, HB:HBP, :] = jnp.zeros((HBP - HB, TOK), BF16)
-        fcg_all[s, HG:HGP, :] = jnp.zeros((HGP - HG, TOK), BF16)
     proj_b[HB:HBP, :] = jnp.zeros((HBP - HB, WB), BF16)
     loads["mod_b"].wait()
     mods = pad_rows(
@@ -254,8 +247,6 @@
     mean = jnp.sum(dev_b[...], axis=0, keepdims=True) * (1.0 / WB)
     dev_b[...] -= mean
     means[j] = jnp.broadcast_to(mean, (8, TOK))
-    for n in range(1, 8):
-        go(remote(means.at[j], means.at[j], mn_send, mn_recv, {"tp": tp_peer(n)}))
     loads["proj_b"].wait()
     for q in range(NC):
         proj_bt[128 * q : 128 * q + 128, :] = proj_b[:, 128 * q : 128 * q + 128].T
@@ -307,6 +298,9 @@
         hidden_copy(s, h, k, target).start()
 
     def scale_all():
+        seven(cots, cot_send, cot_recv).wait_recv()
+        seven(means, mn_send, mn_recv).wait_recv()
+
         def one(d, carry):
             scaled_b[d] = (
                 jnp.dot(head_bt[...], pad_rows(cots[d], 128), preferred_element_type=F32) * scale_b[...]
@@ -350,7 +344,28 @@
         for n in range(1, 8):
             fcg_copy(me, n, seq_peer(n), fc_g).start()
 
+    def share():
+        loads["cot"].wait()
+        cot = cot_ref[...]
+        cots[j] = (strength * cot).astype(BF16)
+        for n in range(1, 8):
+            go(remote(cots.at[j], cots.at[j], cot_send, cot_recv, {"tp": tp_peer(n)}))
+        for n in range(1, 8):
+            go(remote(means.at[j], means.at[j], mn_send, mn_recv, {"tp": tp_peer(n)}))
+
+    def prepare():
+        for s in range(8):
+            fcg_all[s, HG:HGP, :] = jnp.zeros((HGP - HG, TOK), BF16)
+        loads["head_b"].wait()
+        head_bt[...] = pad_lanes(head_b[...].T, 128)
+        loads["proj_g"].wait()
+        proj_gp[...] = pad_lanes(proj_g[...], HGP)
+        loads["fcg"].wait()
+        head_sum[...] = jnp.zeros_like(head_sum)
+
     events = (
+        (1, share),
+        (3, prepare),
         (NQ, beside),
         (2 * NQ - 2, near),
         (2 * NQ, near_rest),
@@ -414,7 +429,6 @@
         return inverse, offset, inverse * inverse * second, inverse * (first + offset * second)
 
     def consume(d):
-        d = jnp.int32(d)
         b = place_of(d)
         seven(stats.at[d], st_send, st_recv.at[d]).wait_recv()
         every = [stats[d, s] for s in range(8)]
@@ -520,12 +534,6 @@
             def _():
                 out_copy(b, q).start()
 
-            for d, (at_b, at_q) in enumerate(((6, 3), (7, 0), (7, 1), (7, 2))):
-
-                @pl.when((b == at_b) & (q == at_q))
-                def _():
-                    consume(d)
-
             @pl.when(q == NQ - 1)
             def _():
                 block_stats(block_at(b), b)
@@ -536,18 +544,12 @@
     def add(a, b):
         return (a.astype(F32) + b.astype(F32)).astype(BF16)
 
-    loads["head_b"].wait()
-    head_bt[...] = pad_lanes(head_b[...].T, 128)
-    loads["proj_g"].wait()
-    proj_gp[...] = pad_lanes(proj_g[...], HGP)
-    loads["fcg"].wait()
-    head_sum[...] = jnp.zeros_like(head_sum)
-    seven(cots, cot_send, cot_recv).wait_recv()
-    seven(means, mn_send, mn_recv).wait_recv()
-
     lax.fori_loop(0, UNITS + 7 * SKEW, tick, 0)
-    for d in range(4, 8):
+    def consume_one(d, carry):
         consume(d)
+        return carry
+
+    lax.fori_loop(0, 8, consume_one, 0)
 
     def rows(shard):
         return pl.ds(pl.multiple_of(shard * SHARD, 16), SHARD)

time: 132 us -> 124 us (0.939)
  Pallas kernels: 126 us -> 118 us
    pallas_call x1, Pallas kernels: 126 us -> 118 us  [shards(): pl.pallas_call(kernel, out_shape=tuple((V(*s) for s in shapes)), in_specs...]
where the time goes in v4:
time: 124 us
  Pallas kernels  118 us (95%)
  local copies, waits for them, and re-layouts  3.56 us (3%)
  between operations  1.94 us (2%)
    pallas_call x1, Pallas kernels, shards(): pl.pallas_call(kernel, out_shape=tuple((V(*s) for s in shapes)), in_specs...  118 us
    unnamed x5, local copies, waits for them, and re-layouts  3.56 us

profile of v4, /device:TPU:24, one launch (start us, length us, event | category | flops | bytes accessed | tf_op | source)
XLA Modules:
  0.0 123.9 jit_solution(13505321245130777156)
XLA Ops:
  1.9 118.4 %shard_map.173 = (f32[64,128]{1,0:T(8,128)S(1)}, bf16[864,640]{1,0:T(8,128)(2,1)S(1)}, f32[64,640]{1,0:T(8,128)S(1)}, bf16[128,640]{1,0:T(8,128)(2,1)S(1)}, bf16[192,128]{1,0:T(8,128)(2,1)S(1)}) custom-call(s32[1]{0:T(128)S(6)} %copy.29.time_ref, s32[1]{0:T(128)S(6)} %copy.30.level_ref, f32[8]{0:T(128)} %table_ref.1, bf16[864,128]{1,0:T(8,128)(2,1)} %bitcast.17, ...), custom_call_target="tpu_custom_call" | custom-call | tf_op jit(solution)/shard_map/pallas_call | solution.py:795
  120.3 0.6 copy.24
  120.9 0.6 copy.28
  121.5 0.7 copy.26
  122.2 0.7 copy.27
  122.9 1.0 copy.25
